TPU v7x, 512 devices: a whole 4x4x16 slice. The times are simulated.
512 devices in a mesh: xy: 64 (over y, z), gz: 8 (over x, core).
Axes of the slice: x: 4, y: 4, z: 16, core: 2. Of those that a mesh axis runs over, the one named last changes fastest.
Arguments:
- conc_prev: float32 [4, 16, 1024, 1024], P(None, 'gz', 'xy'), may hold values from 0.5 to 2
- conc_section: float32 [3, 4, 16, 1024, 1024], P(None, None, 'gz', 'xy'), may hold values from 0.5 to 2
- potential: float32 [3, 16, 1024, 1024], P(None, 'gz', 'xy'), may hold values from -6 to 6
- diffusivity: float32 [4], replicated, may hold values from 0.2 to 1
- charges: int32 [4], replicated, may hold values from -2 to 2, as said below
Outputs:
- conc_new: float32 [3, 4, 16, 1024, 1024], P(None, None, 'gz', 'xy')
- potential_new: float32 [3, 16, 1024, 1024], P(None, 'gz', 'xy')
Inputs may be any that keep to these rules, and one draw needn't show every extreme that they name: Each charge is plus or minus 1 or 2, and the 4 charges sum to zero.
All inputs are finite; a program needn't handle non-finite values.
Results may differ from a plain program's by a relative error of at most 0.00027.
Values sent between devices are 32-bit elements; how exact they have to be, the bound alone decides.
No kernel may reach another device: no remote copies, remote signals or barrier semaphores. Data moves between devices by JAX's collectives and lax.ppermute only.
A program may use at most 64 MiB of HBM per device.

v0:
```python
import math

import jax
import jax.numpy as jnp
import numpy as np
from jax import lax
from jax.experimental import pallas as pl
from jax.experimental.pallas import tpu as pltpu
from jax.sharding import PartitionSpec as P

step_size = 0.2
screening = 0.005
lanes = 128


def radau_matrix():
    root = math.sqrt(6.0)
    return [
        [(88.0 - 7.0 * root) / 360.0, (296.0 - 169.0 * root) / 1800.0, (-2.0 + 3.0 * root) / 225.0],
        [(296.0 + 169.0 * root) / 1800.0, (88.0 + 7.0 * root) / 360.0, (-2.0 - 3.0 * root) / 225.0],
        [(16.0 - root) / 36.0, (16.0 + root) / 36.0, 1.0 / 9.0],
    ]


def cas_halves(length, scale):
    index = np.arange(length)
    angle = (index[:, None] * index[None, :] % length) * (2.0 * math.pi / length)
    table = ((np.cos(angle) + np.sin(angle)) * scale).astype(np.float32)
    high = table.astype(jnp.bfloat16)
    low = (table - high.astype(np.float32)).astype(jnp.bfloat16)
    return high, low


def sine_matrix(depth):
    k = np.arange(1, depth + 1)
    return math.sqrt(2.0 / (depth + 1)) * np.sin(np.outer(k, k) * math.pi / (depth + 1))


def decay_tables(depth, y_cells, x_cells, block):
    ez = 2.0 - 2.0 * np.cos(np.arange(1, depth + 1) * math.pi / (depth + 1))
    ey = 2.0 - 2.0 * np.cos(np.arange(y_cells) * 2.0 * math.pi / y_cells)
    lam = screening + ez[:, None] + ey[None, :]
    root = np.sqrt(lam + 0.25 * lam * lam)
    r = 1.0 / (1.0 + 0.5 * lam + root)
    return np.stack([r, 0.5 / root, r**block, 1.0 / (1.0 - r**x_cells)]).astype(np.float32)


def face(near, far, gain):
    return (far - near) + gain * (near + far)


def split_dot(rows, high_ref, low_ref):
    high = rows.astype(jnp.bfloat16)
    low = (rows - high.astype(jnp.float32)).astype(jnp.bfloat16)

    def product(a, b):
        return jnp.dot(a, b, preferred_element_type=jnp.float32)

    return product(high, low_ref[...]) + product(low, high_ref[...]) + product(high, high_ref[...])


def inner_kernel(coef_ref, inv_ref, half_ref, prev_ref, conc_ref, pot_ref, left_ref, right_ref, out_ref):
    n_section, n_species, depth, rows, y_cells = conc_ref.shape
    row = lax.broadcasted_iota(jnp.int32, (rows, y_cells), 0)

    def species(s, carry):
        half = half_ref[s]
        totals = []
        for j in range(n_section):
            planes = []
            for z in range(depth):
                c = conc_ref[j, s, z]
                p = pot_ref[j, z]
                edge = left_ref[j, s, z]
                edge_p = left_ref[j, n_species, z]
                c_before = jnp.where(row == 0, edge, pltpu.roll(c, 1, 0))
                p_before = jnp.where(row == 0, edge_p, pltpu.roll(p, 1, 0))
                low = face(c_before, c, half * (p - p_before))
                c_last = c[rows - 1 :]
                p_last = p[rows - 1 :]
                last = face(
                    c_last, right_ref[j, s, z], half * (right_ref[j, n_species, z] - p_last)
                )
                high = jnp.where(row == rows - 1, last, pltpu.roll(low, rows - 1, 0))
                c_next = pltpu.roll(c, y_cells - 1, 1)
                p_next = pltpu.roll(p, y_cells - 1, 1)
                ahead = face(c, c_next, half * (p_next - p))
                planes.append((high - low) + (ahead - pltpu.roll(ahead, 1, 1)))
            between = face(conc_ref[j, s, 0], conc_ref[j, s, 1], half * (pot_ref[j, 1] - pot_ref[j, 0]))
            totals.append((planes[0] + between, planes[1] - between))
        for z in range(depth):
            for i in range(n_section):
                c = conc_ref[i, s, z]
                update = inv_ref[i * n_species + s] * (prev_ref[s, z] - c)
                for j in range(n_section):
                    update = update + coef_ref[(i * n_section + j) * n_species + s] * totals[j][z]
                out_ref[i, s, z] = c + update
        return carry

    lax.fori_loop(0, n_species, species, 0)


def outer_kernel(
    coef_ref, half_ref, part_ref, conc_ref, pot_ref, below_ref, above_ref, high_ref, low_ref,
    out_ref, modes_ref, rhs_ref,
):
    n_section, n_species, depth, rows, y_cells = conc_ref.shape
    for i in range(n_section):
        for z in range(depth):
            rhs_ref[i, z] = screening * pot_ref[i, z]

    def species(s, carry):
        half = half_ref[s]
        for z in range(depth):
            faces = []
            for j in range(n_section):
                c = conc_ref[j, s, z]
                p = pot_ref[j, z]
                if z == 0:
                    far, far_p = below_ref[j, s], below_ref[j, n_species]
                else:
                    far, far_p = above_ref[j, s], above_ref[j, n_species]
                faces.append(face(c, far, half * (far_p - p)))
            for i in range(n_section):
                update = part_ref[i, s, z]
                for j in range(n_section):
                    update = update + coef_ref[(i * n_section + j) * n_species + s] * faces[j]
                out_ref[i, s, z] = update
                rhs_ref[i, z] += (2.0 * half) * update
        return carry

    lax.fori_loop(0, n_species, species, 0)
    rhs = rhs_ref[...].reshape(n_section * depth * rows, y_cells)
    modes = split_dot(rhs, high_ref, low_ref)
    for g in range(y_cells // lanes):
        modes_ref[g] = modes[:, g * lanes : (g + 1) * lanes].reshape(n_section, depth, rows, lanes)


def sine_rows(planes, table):
    depth = len(planes)
    half = depth // 2
    even = [planes[z] + planes[depth - 1 - z] for z in range(half)]
    odd = [planes[z] - planes[depth - 1 - z] for z in range(half)]
    out = []
    for k in range(depth):
        source = even if k % 2 == 0 else odd
        total = source[0] * float(table[k, 0])
        for z in range(1, half):
            total = total + source[z] * float(table[k, z])
        out.append(total)
    return out


def sum_kernel(table, decay_ref, modes_ref, hat_ref, sums_ref, rows_ref):
    n_gz, n_section, n_z, rows, _ = modes_ref.shape
    depth = n_gz * n_z
    r = decay_ref[0]
    sums_ref[...] = jnp.zeros_like(sums_ref)
    for i in range(n_section):
        planes = [modes_ref[z // n_z, i, z % n_z] for z in range(depth)]
        for k, plane in enumerate(sine_rows(planes, table)):
            rows_ref[i, pl.ds(k * rows, rows), :] = plane
        for x in range(rows):
            hat_ref[i, x] = rows_ref[i, pl.ds(x, depth, stride=rows), :]
        ahead = hat_ref[i, 0]
        back = hat_ref[i, rows - 1]
        for x in range(1, rows):
            ahead = ahead * r + hat_ref[i, x]
            back = back * r + hat_ref[i, rows - 1 - x]
        sums_ref[pl.ds(i * 2 * depth, depth, stride=2), :] = ahead
        sums_ref[pl.ds(i * 2 * depth + 1, depth, stride=2), :] = back


def ring_kernel(rho_ref, scale_ref, sums_ref, out_ref):
    n_xy = sums_ref.shape[0] // 2
    rho = rho_ref[...]
    ahead = sums_ref[0:1, :]
    back = sums_ref[2 * n_xy - 1 : 2 * n_xy, :]
    for d in range(1, n_xy):
        ahead = ahead * rho + sums_ref[2 * d : 2 * d + 1, :]
        e = n_xy - 1 - d
        back = back * rho + sums_ref[2 * e + 1 : 2 * e + 2, :]
    ahead = ahead * scale_ref[...]
    back = back * scale_ref[...]
    for d in range(n_xy):
        out_ref[2 * d : 2 * d + 1, :] = ahead
        ahead = ahead * rho + sums_ref[2 * d : 2 * d + 1, :]
        e = n_xy - 1 - d
        out_ref[2 * e + 1 : 2 * e + 2, :] = back
        back = back * rho + sums_ref[2 * e + 1 : 2 * e + 2, :]


def solve_kernel(table, decay_ref, hat_ref, enter_ref, out_ref, work_ref, rows_ref):
    n_gz, n_section, n_z, rows, _ = out_ref.shape
    depth = n_gz * n_z
    r = decay_ref[0]
    inverse = decay_ref[1]
    for i in range(n_section):
        value = enter_ref[pl.ds(i * 2 * depth, depth, stride=2), :]
        for x in range(rows):
            source = hat_ref[i, x]
            work_ref[x] = value * r
            value = value * r + source
        value = enter_ref[pl.ds(i * 2 * depth + 1, depth, stride=2), :]
        for x in range(rows - 1, -1, -1):
            value = value * r + hat_ref[i, x]
            rows_ref[i, pl.ds(x, depth, stride=rows), :] = (work_ref[x] + value) * inverse
        planes = [rows_ref[i, pl.ds(k * rows, rows), :] for k in range(depth)]
        for z, plane in enumerate(sine_rows_back(planes, table)):
            out_ref[z // n_z, i, z % n_z] = plane


def sine_rows_back(planes, table):
    depth = len(planes)
    out = [None] * depth
    for z in range(depth // 2):
        parts = []
        for parity in range(2):
            total = planes[parity] * float(table[parity, z])
            for k in range(parity + 2, depth, 2):
                total = total + planes[k] * float(table[k, z])
            parts.append(total)
        out[z] = parts[0] + parts[1]
        out[depth - 1 - z] = parts[0] - parts[1]
    return out


def final_kernel(solved_ref, high_ref, low_ref, out_ref):
    n_gz, n_section, n_z, rows, _ = solved_ref.shape
    modes = jnp.concatenate(
        [solved_ref[g].reshape(n_section * n_z * rows, lanes) for g in range(n_gz)], axis=1
    )
    field = split_dot(modes, high_ref, low_ref)
    out_ref[...] = field.reshape(out_ref.shape)


def on_device(conc_prev, conc_section, potential, diffusivity, charges):
    n_xy = lax.axis_size("xy")
    n_gz = lax.axis_size("gz")
    n_section, n_species, n_z, rows, y_cells = conc_section.shape
    depth = n_z * n_gz
    x_cells = rows * n_xy
    f32 = jnp.float32
    vmem = pl.BlockSpec(memory_space=pltpu.VMEM)
    smem = pl.BlockSpec(memory_space=pltpu.SMEM)
    params = pltpu.CompilerParams(vmem_limit_bytes=40 * 1024 * 1024)
    forward_high, forward_low = cas_halves(y_cells, 1.0 / 32.0)
    sine = sine_matrix(depth)
    decay = jnp.asarray(decay_tables(depth, y_cells, x_cells, rows))

    top = jnp.concatenate([conc_section[:, :, -1], potential[:, None, -1]], axis=1)
    bottom = jnp.concatenate([conc_section[:, :, 0], potential[:, None, 0]], axis=1)
    last = jnp.concatenate([conc_section[:, :, :, -1:], potential[:, None, :, -1:]], axis=1)
    first = jnp.concatenate([conc_section[:, :, :, :1], potential[:, None, :, :1]], axis=1)
    below = lax.ppermute(top, "gz", [(i, i + 1) for i in range(n_gz - 1)])
    above = lax.ppermute(bottom, "gz", [(i + 1, i) for i in range(n_gz - 1)])
    left = lax.ppermute(last, "xy", [(i, (i + 1) % n_xy) for i in range(n_xy)])
    right = lax.ppermute(first, "xy", [((i + 1) % n_xy, i) for i in range(n_xy)])

    butcher = np.asarray(radau_matrix(), np.float32)
    scale_row = 1.0 / (
        1.0 + 6.0 * step_size * np.diag(butcher)[:, None] * diffusivity[None, :]
    )
    coef = (step_size * butcher)[:, :, None] * (diffusivity[None, :] * scale_row)[:, None, :]
    half = 0.5 * charges.astype(f32)
    coef = coef.reshape(-1)

    z_index = lax.axis_index("gz")
    decay_here = lax.dynamic_slice_in_dim(decay, z_index * lanes, lanes, 2)
    kz_here = lax.axis_index("xy") % depth
    rho_here = lax.dynamic_slice_in_dim(decay_here[2], kz_here, 1, 0)
    scale_here = lax.dynamic_slice_in_dim(decay_here[3], kz_here, 1, 0)

    part = pl.pallas_call(
        inner_kernel,
        out_shape=jax.ShapeDtypeStruct(conc_section.shape, f32),
        in_specs=[smem] * 3 + [vmem] * 5,
        out_specs=vmem,
        compiler_params=params,
        cost_estimate=pl.CostEstimate(flops=20_000_000, bytes_accessed=4_500_000, transcendentals=0),
        name="inner_faces",
    )(coef, scale_row.reshape(-1), half, conc_prev, conc_section, potential, left, right)

    conc_new, modes = pl.pallas_call(
        outer_kernel,
        out_shape=(
            jax.ShapeDtypeStruct(conc_section.shape, f32),
            jax.ShapeDtypeStruct((n_gz, n_section, n_z, rows, lanes), f32),
        ),
        in_specs=[smem] * 2 + [vmem] * 7,
        out_specs=(vmem, vmem),
        scratch_shapes=[pltpu.VMEM((n_section, n_z, rows, y_cells), f32)],
        input_output_aliases={2: 0},
        compiler_params=params,
        name="outer_faces",
    )(coef, half, part, conc_section, potential, below, above, forward_high, forward_low)

    columns = lax.all_to_all(modes, "gz", split_axis=0, concat_axis=0, tiled=True)

    n_rows = 2 * n_xy
    hat, sums = pl.pallas_call(
        lambda *refs: sum_kernel(sine, *refs),
        out_shape=(
            jax.ShapeDtypeStruct((n_section, rows, depth, lanes), f32),
            jax.ShapeDtypeStruct((n_rows, lanes), f32),
        ),
        in_specs=[vmem] * 2,
        out_specs=(vmem, vmem),
        scratch_shapes=[pltpu.VMEM((n_section, depth * rows, lanes), f32)],
        compiler_params=params,
        name="block_sums",
    )(decay_here, columns)

    gathered = lax.all_to_all(sums, "xy", split_axis=0, concat_axis=0, tiled=True)
    entering = pl.pallas_call(
        ring_kernel,
        out_shape=jax.ShapeDtypeStruct((n_rows, lanes), f32),
        in_specs=[vmem] * 3,
        out_specs=vmem,
        compiler_params=params,
        name="ring",
    )(rho_here, scale_here, gathered)
    enter = lax.all_to_all(entering, "xy", split_axis=0, concat_axis=0, tiled=True)

    solved = pl.pallas_call(
        lambda *refs: solve_kernel(sine, *refs),
        out_shape=jax.ShapeDtypeStruct((n_gz, n_section, n_z, rows, lanes), f32),
        in_specs=[vmem] * 3,
        out_specs=vmem,
        scratch_shapes=[
            pltpu.VMEM((rows, depth, lanes), f32),
            pltpu.VMEM((n_section, depth * rows, lanes), f32),
        ],
        compiler_params=params,
        name="solve",
    )(decay_here, hat, enter)
    returned = lax.all_to_all(solved, "gz", split_axis=0, concat_axis=0, tiled=True)

    potential_new = pl.pallas_call(
        final_kernel,
        out_shape=jax.ShapeDtypeStruct(potential.shape, f32),
        in_specs=[vmem] * 3,
        out_specs=vmem,
        compiler_params=params,
        name="back_to_y",
    )(returned, forward_high, forward_low)
    return (conc_new, potential_new)


def solution(mesh):
    in_specs = (
        P(None, "gz", "xy", None),
        P(None, None, "gz", "xy", None),
        P(None, "gz", "xy", None),
        P(),
        P(),
    )
    out_specs = (P(None, None, "gz", "xy", None), P(None, "gz", "xy", None))
    return jax.shard_map(
        on_device, mesh=mesh, in_specs=in_specs, out_specs=out_specs, check_vma=False
    )
```

profile of v0, /device:TPU:1, one launch (start us, length us, event | category | flops | bytes accessed | tf_op | source)
XLA Modules:
  0.0 115.8 jit_solution(6641314650203727309)
XLA Ops:
  0.6 1.1 fusion.1
  1.7 1.5 %slice_bitcast_fusion = (f32[3,4,16,1024]{3,2,1,0:T(8,128)S(1)}, f32[3,4,16,1024]{3,2,1,0:T(8,128)S(1)}) fusion(f32[3,4,2,16,1024]{4,3,2,1,0:T(8,128)} %conc_ref.3), kind=kLoop, calls=%fused_computation.2 | loop fusion | bytes 3145728 | tf_op jit(solution)/shard_map/squeeze | solution.py:252
  3.2 1.0 pad_maximum_fusion
  4.3 4.6 %collective-permute-start.2 = (f32[3,5,16,1024]{3,2,1,0:T(8,128)}, f32[3,5,16,1024]{3,2,1,0:T(8,128)S(1)}, u32[]{:S(2)}, u32[]{:S(2)}) collective-permute-start(f32[3,5,16,1024]{3,2,1,0:T(8,128)} %pad_maximum_fusion), channel_id=1, source_target_pairs={{0,1},{1,2},{2,3},{3,4},{4,5},{5,6},{6,7},{8,9},{9,10},{10,11},{11... | collective-permute-start | bytes 2949128 | tf_op jit(solution)/shard_map/ppermute | solution.py:255
  8.9 1.0 pad_maximum_fusion.1
  9.9 5.6 %collective-permute-start.3 = (f32[3,5,16,1024]{3,2,1,0:T(8,128)}, f32[3,5,16,1024]{3,2,1,0:T(8,128)}, u32[]{:S(2)}, u32[]{:S(2)}) collective-permute-start(f32[3,5,16,1024]{3,2,1,0:T(8,128)} %pad_maximum_fusion.1), channel_id=1, source_target_pairs={{1,0},{2,1},{3,2},{4,3},{5,4},{6,5},{7,6},{9,8},{10,9},{11,10},{12... | collective-permute-start | bytes 2949128 | tf_op jit(solution)/shard_map/ppermute | solution.py:256
  15.8 0.8 pad_maximum_fusion.2
  16.5 1.9 %collective-permute-start = (f32[3,5,2,1,1024]{4,3,2,1,0:T(1,128)}, f32[3,5,2,1,1024]{4,3,2,1,0:T(1,128)}, u32[]{:S(2)}, u32[]{:S(2)}) collective-permute-start(f32[3,5,2,1,1024]{4,3,2,1,0:T(1,128)} %pad_maximum_fusion.2), channel_id=1, source_target_pairs={{0,8},{8,16},{16,24},{24,32},{32,40},{40,48},{48,56},{56,64},{64,7... | collective-permute-start | bytes 368648 | tf_op jit(solution)/shard_map/ppermute | solution.py:257
  18.5 0.8 pad_maximum_fusion.3
  19.2 9.9 %collective-permute-start.1 = (f32[3,5,2,1,1024]{4,3,2,1,0:T(1,128)}, f32[3,5,2,1,1024]{4,3,2,1,0:T(1,128)}, u32[]{:S(2)}, u32[]{:S(2)}) collective-permute-start(f32[3,5,2,1,1024]{4,3,2,1,0:T(1,128)} %pad_maximum_fusion.3), channel_id=1, source_target_pairs={{8,0},{16,8},{24,16},{32,24},{40,32},{48,40},{56,48},{64,56},{72,6... | collective-permute-start | bytes 368648 | tf_op jit(solution)/shard_map/ppermute | solution.py:258
  29.5 1.8 %collective-permute-done.1.right_ref = f32[3,5,2,1,1024]{4,3,2,1,0:T(1,128)} collective-permute-done((f32[3,5,2,1,1024]{4,3,2,1,0:T(1,128)}, f32[3,5,2,1,1024]{4,3,2,1,0:T(1,128)}, u32[]{:S(2)}, u32[]{:S(2)}) %collective-permute-start.1) | collective-permute-done | bytes 122912 | tf_op jit(solution)/shard_map/ppermute | solution.py:258
  31.3 4.9 %inner_faces.1.part_ref = f32[3,4,2,16,1024]{4,3,2,1,0:T(8,128)} custom-call(f32[36]{0:T(128)S(1)} %mul.65.coef_ref, f32[12]{0:T(128)S(1)} %div.12.inv_ref, f32[4]{0:T(128)S(1)} %convert_multiply_fusion.half_ref, f32[4,2,16,1024]{3,2,1,0:T(8,128)S(1)} %copy-done.6, f32[3,4,2,16,1024]{4,3,2,1,0:T(8,128)S(1)} %copy-done, f32[3,2,16,1024]{3,2,1,0:T(8,128)S(1)} %copy-done.5, ...), custom_call_target="tpu_custom_call" | custom-call | flops 20000000 | bytes 4500000 | tf_op jit(solution)/shard_map/inner_faces/pallas_call | solution.py:274
  36.2 4.4 %outer_faces.1 = (f32[3,4,2,16,1024]{4,3,2,1,0:T(8,128)}, f32[8,3,2,16,128]{4,3,2,1,0:T(8,128)}) custom-call(f32[36]{0:T(128)S(1)} %mul.65.coef_ref, f32[4]{0:T(128)S(1)} %convert_multiply_fusion.half_ref, f32[3,4,2,16,1024]{4,3,2,1,0:T(8,128)} %inner_faces.1.part_ref, f32[3,4,2,16,1024]{4,3,2,1,0:T(8,128)S(1)} %copy-done, ...), custom_call_target="tpu_custom_call", output_to_operand_aliasing={{0}: (2, {})} | custom-call | tf_op jit(solution)/shard_map/outer_faces/pallas_call | solution.py:284
  40.6 5.9 %all-to-all-start = ((f32[8,3,2,16,128]{4,3,2,1,0:T(8,128)}), f32[8,3,2,16,128]{4,3,2,1,0:T(8,128)S(1)}, u32[]{:S(2)}, u32[]{:S(2)}) async-start(f32[8,3,2,16,128]{4,3,2,1,0:T(8,128)} %get-tuple-element.7), calls=%async_computation | async-start | bytes 786432 | tf_op jit(solution)/shard_map/all_to_all | solution.py:298
  46.6 0.8 constant_dynamic-slice_fusion.refs_0_
  47.3 7.3 %all-to-all-done.refs_1_ = f32[8,3,2,16,128]{4,3,2,1,0:T(8,128)S(1)} async-done(((f32[8,3,2,16,128]{4,3,2,1,0:T(8,128)}), f32[8,3,2,16,128]{4,3,2,1,0:T(8,128)S(1)}, u32[]{:S(2)}, u32[]{:S(2)}) %all-to-all-start) | async-done | bytes 393248 | tf_op jit(solution)/shard_map/all_to_all | solution.py:298
  54.6 1.0 block_sums.1
  55.6 10.7 %all-to-all-start.1 = ((f32[64,2,128]{2,1,0:T(2,128)}), f32[64,2,128]{2,1,0:T(2,128)S(1)}, u32[]{:S(2)}, u32[]{:S(2)}) async-start(f32[64,2,128]{2,1,0:T(2,128)} %bitcast.6), calls=%async_computation.1 | async-start | bytes 131072 | tf_op jit(solution)/shard_map/all_to_all | solution.py:314
  66.4 0.8 dynamic-slice_bitcast_fusion
  67.2 12.7 %all-to-all-done.1 = f32[64,2,128]{2,1,0:T(2,128)S(1)} async-done(((f32[64,2,128]{2,1,0:T(2,128)}), f32[64,2,128]{2,1,0:T(2,128)S(1)}, u32[]{:S(2)}, u32[]{:S(2)}) %all-to-all-start.1) | async-done | bytes 65568 | tf_op jit(solution)/shard_map/all_to_all | solution.py:314
  80.2 17.8 %all_to_all.32 = f32[64,2,128]{2,1,0:T(2,128)S(1)} all-to-all(f32[64,2,128]{2,1,0:T(2,128)S(1)} %bitcast.22), channel_id=1, replica_groups=mesh['xy'=64,'gz'=8] {'xy'}, dimensions={0} | all-to-all | bytes 131072 | tf_op jit(solution)/shard_map/all_to_all | solution.py:323
  98.4 14.0 %all_to_all.33.solved_ref = f32[8,3,2,16,128]{4,3,2,1,0:T(8,128)S(1)} all-to-all(f32[8,3,2,16,128]{4,3,2,1,0:T(8,128)S(1)} %solve.1), channel_id=1, replica_groups=mesh['xy'=64,'gz'=8] {'gz'}, dimensions={0} | all-to-all | bytes 786432 | tf_op jit(solution)/shard_map/all_to_all | solution.py:337
  112.4 1.6 %copy-done.4 = bf16[1024,1024]{1,0:T(8,128)(2,1)S(1)} copy-done((bf16[1024,1024]{1,0:T(8,128)(2,1)S(1)}, bf16[1024,1024]{1,0:T(8,128)(2,1)}, u32[]{:S(2)}) %copy-start.4) | copy-done | bytes 2097176
  114.0 1.9 %back_to_y.1 = f32[3,2,16,1024]{3,2,1,0:T(8,128)} custom-call(f32[8,3,2,16,128]{4,3,2,1,0:T(8,128)S(1)} %all_to_all.33.solved_ref, bf16[1024,1024]{1,0:T(8,128)(2,1)S(1)} %copy-done.2, bf16[1024,1024]{1,0:T(8,128)(2,1)S(1)} %copy-done.4), custom_call_target="tpu_custom_call" | custom-call | tf_op jit(solution)/shard_map/back_to_y/pallas_call | solution.py:339
  (33 shorter events, 1.2 us)
Async XLA Ops:
  3.2 12.4 %copy-start = (f32[3,4,2,16,1024]{4,3,2,1,0:T(8,128)S(1)}, f32[3,4,2,16,1024]{4,3,2,1,0:T(8,128)}, u32[]{:S(2)}) copy-start(f32[3,4,2,16,1024]{4,3,2,1,0:T(8,128)} %conc_ref.3) | copy-start | bytes 4718596
  4.2 11.5 %copy-start.5 = (f32[3,2,16,1024]{3,2,1,0:T(8,128)S(1)}, f32[3,2,16,1024]{3,2,1,0:T(8,128)}, u32[]{:S(2)}) copy-start(f32[3,2,16,1024]{3,2,1,0:T(8,128)} %pot_ref.3) | copy-start | bytes 1179652
  4.2 24.9 %copy-start.8 = (f32[4]{0:T(128)S(1)}, f32[4]{0:T(128)}, u32[]{:S(2)}) copy-start(f32[4]{0:T(128)} %param.13) | copy-start | bytes 52
  4.2 24.9 %copy-start.9 = (f32[3]{0:T(128)S(1)}, f32[3]{0:T(128)}, u32[]{:S(2)}) copy-start(f32[3]{0:T(128)} %constant.52) | copy-start | bytes 40
  4.2 25.0 %copy-start.7 = (f32[3,3]{1,0:T(4,128)S(1)}, f32[3,3]{1,0:T(4,128)}, u32[]{:S(2)}) copy-start(f32[3,3]{1,0:T(4,128)} %constant.51) | copy-start | bytes 112
  4.2 25.2 %copy-start.10 = (s32[4]{0:T(128)S(1)}, s32[4]{0:T(128)}, u32[]{:S(2)}) copy-start(s32[4]{0:T(128)} %param.14) | copy-start | bytes 52
  4.3 27.0 %copy-start.6 = (f32[4,2,16,1024]{3,2,1,0:T(8,128)S(1)}, f32[4,2,16,1024]{3,2,1,0:T(8,128)}, u32[]{:S(2)}) copy-start(f32[4,2,16,1024]{3,2,1,0:T(8,128)} %prev_ref.1) | copy-start | bytes 1572868
  4.3 31.9 %collective-permute-start.2 = (f32[3,5,16,1024]{3,2,1,0:T(8,128)}, f32[3,5,16,1024]{3,2,1,0:T(8,128)S(1)}, u32[]{:S(2)}, u32[]{:S(2)}) collective-permute-start(f32[3,5,16,1024]{3,2,1,0:T(8,128)} %pad_maximum_fusion), channel_id=1, source_target_pairs={{0,1},{1,2},{2,3},{3,4},{4,5},{5,6},{6,7},{8,9},{9,10},{10,11},{11... | collective-permute-start | bytes 2949128 | tf_op jit(solution)/shard_map/ppermute | solution.py:255
  9.9 26.3 %collective-permute-start.3 = (f32[3,5,16,1024]{3,2,1,0:T(8,128)}, f32[3,5,16,1024]{3,2,1,0:T(8,128)}, u32[]{:S(2)}, u32[]{:S(2)}) collective-permute-start(f32[3,5,16,1024]{3,2,1,0:T(8,128)} %pad_maximum_fusion.1), channel_id=1, source_target_pairs={{1,0},{2,1},{3,2},{4,3},{5,4},{6,5},{7,6},{9,8},{10,9},{11,10},{12... | collective-permute-start | bytes 2949128 | tf_op jit(solution)/shard_map/ppermute | solution.py:256
  16.5 12.9 %collective-permute-start = (f32[3,5,2,1,1024]{4,3,2,1,0:T(1,128)}, f32[3,5,2,1,1024]{4,3,2,1,0:T(1,128)}, u32[]{:S(2)}, u32[]{:S(2)}) collective-permute-start(f32[3,5,2,1,1024]{4,3,2,1,0:T(1,128)} %pad_maximum_fusion.2), channel_id=1, source_target_pairs={{0,8},{8,16},{16,24},{24,32},{32,40},{40,48},{48,56},{56,64},{64,7... | collective-permute-start | bytes 368648 | tf_op jit(solution)/shard_map/ppermute | solution.py:257
  19.2 12.0 %collective-permute-start.1 = (f32[3,5,2,1,1024]{4,3,2,1,0:T(1,128)}, f32[3,5,2,1,1024]{4,3,2,1,0:T(1,128)}, u32[]{:S(2)}, u32[]{:S(2)}) collective-permute-start(f32[3,5,2,1,1024]{4,3,2,1,0:T(1,128)} %pad_maximum_fusion.3), channel_id=1, source_target_pairs={{8,0},{16,8},{24,16},{32,24},{40,32},{48,40},{56,48},{64,56},{72,6... | collective-permute-start | bytes 368648 | tf_op jit(solution)/shard_map/ppermute | solution.py:258
  29.4 6.8 %copy-start.1 = (bf16[1024,1024]{1,0:T(8,128)(2,1)S(1)}, bf16[1024,1024]{1,0:T(8,128)(2,1)}, u32[]{:S(2)}) copy-start(bf16[1024,1024]{1,0:T(8,128)(2,1)} %constant.46.clone.high_ref) | copy-start | bytes 6291460
  29.4 6.8 %copy-start.3 = (bf16[1024,1024]{1,0:T(8,128)(2,1)S(1)}, bf16[1024,1024]{1,0:T(8,128)(2,1)}, u32[]{:S(2)}) copy-start(bf16[1024,1024]{1,0:T(8,128)(2,1)} %constant.47.clone.low_ref) | copy-start | bytes 6291460
  40.6 71.7 %copy-start.2 = (bf16[1024,1024]{1,0:T(8,128)(2,1)S(1)}, bf16[1024,1024]{1,0:T(8,128)(2,1)}, u32[]{:S(2)}) copy-start(bf16[1024,1024]{1,0:T(8,128)(2,1)} %constant.46.clone.high_ref) | copy-start | bytes 6291460
  40.6 14.0 %all-to-all-start = ((f32[8,3,2,16,128]{4,3,2,1,0:T(8,128)}), f32[8,3,2,16,128]{4,3,2,1,0:T(8,128)S(1)}, u32[]{:S(2)}, u32[]{:S(2)}) async-start(f32[8,3,2,16,128]{4,3,2,1,0:T(8,128)} %get-tuple-element.7), calls=%async_computation | async-start | bytes 786432 | tf_op jit(solution)/shard_map/all_to_all | solution.py:298
  55.6 24.2 %all-to-all-start.1 = ((f32[64,2,128]{2,1,0:T(2,128)}), f32[64,2,128]{2,1,0:T(2,128)S(1)}, u32[]{:S(2)}, u32[]{:S(2)}) async-start(f32[64,2,128]{2,1,0:T(2,128)} %bitcast.6), calls=%async_computation.1 | async-start | bytes 131072 | tf_op jit(solution)/shard_map/all_to_all | solution.py:314
  112.4 1.6 %copy-start.4 = (bf16[1024,1024]{1,0:T(8,128)(2,1)S(1)}, bf16[1024,1024]{1,0:T(8,128)(2,1)}, u32[]{:S(2)}) copy-start(bf16[1024,1024]{1,0:T(8,128)(2,1)} %constant.47.clone.low_ref) | copy-start | bytes 6291460
where the time goes:
time: 116 us
  starting transfers between devices  38.6 us (33%)
  blocking collectives  31.8 us (27%)
  waiting for transfers between devices  21.8 us (19%)
  Pallas kernels  12.9 us (11%)
  local copies, waits for them, and re-layouts  6.08 us (5%)
  other arithmetic  3.74 us (3%)
    all_to_all x1, blocking collectives, on_device(): lax.all_to_all(entering, 'xy', split_axis=0, concat_axis=0, tiled=True)  17.8 us
    all_to_all x1, blocking collectives, on_device(): lax.all_to_all(solved, 'gz', split_axis=0, concat_axis=0, tiled=True)  14 us
    all_to_all x1, waiting for transfers between devices, on_device(): lax.all_to_all(sums, 'xy', split_axis=0, concat_axis=0, tiled=True)  12.7 us
    all_to_all x1, starting transfers between devices, on_device(): lax.all_to_all(sums, 'xy', split_axis=0, concat_axis=0, tiled=True)  10.7 us
    ppermute x1, starting transfers between devices, on_device(): lax.ppermute(first, 'xy', [((i + 1) % n_xy, i) for i in range(n_xy)])  9.85 us
    all_to_all x1, waiting for transfers between devices, on_device(): lax.all_to_all(modes, 'gz', split_axis=0, concat_axis=0, tiled=True)  7.32 us
    all_to_all x1, starting transfers between devices, on_device(): lax.all_to_all(modes, 'gz', split_axis=0, concat_axis=0, tiled=True)  5.92 us
    ppermute x1, starting transfers between devices, on_device(): above = lax.ppermute(bottom, 'gz', [(i + 1, i) for i in range(n_gz - 1)])  5.62 us
  transfers between devices with their start and end apart: 6, of which 3 were waited for; matrix products, arithmetic and copies ran while one was open for 4% of the time, Pallas kernels for 4%

commit v1 on v0

v1 whole, which is shorter than its diff:
```python
import functools
import math

import jax
import jax.numpy as jnp
import numpy as np
from jax import lax
from jax.experimental import pallas as pl
from jax.experimental.pallas import tpu as pltpu
from jax.sharding import PartitionSpec as P

step_size = 0.2
screening = 0.005
lanes = 128
ring = 16
group = 4
diagonal = math.sqrt(0.5)


def radau_matrix():
    root = math.sqrt(6.0)
    return [
        [(88.0 - 7.0 * root) / 360.0, (296.0 - 169.0 * root) / 1800.0, (-2.0 + 3.0 * root) / 225.0],
        [(296.0 + 169.0 * root) / 1800.0, (88.0 + 7.0 * root) / 360.0, (-2.0 - 3.0 * root) / 225.0],
        [(16.0 - root) / 36.0, (16.0 + root) / 36.0, 1.0 / 9.0],
    ]


def hartley_tables(length):
    b = np.arange(lanes)
    k1 = np.arange(length // lanes)[:, None, None]
    angle = b[:, None] * (k1 + length // lanes * b[None, :]) % length * (2.0 * math.pi / length)
    cas, dif = np.cos(angle) + np.sin(angle), np.sin(angle) - np.cos(angle)
    zero = np.zeros((lanes, lanes))
    pairs = [np.block([[cas[0], zero], [zero, cas[4]]])]
    pairs += [np.block([[cas[p], cas[8 - p]], [dif[p], -dif[8 - p]]]) for p in (1, 2, 3)]
    table = (np.stack(pairs) / math.sqrt(length)).astype(np.float32)
    high = table.astype(jnp.bfloat16)
    low = (table - high.astype(np.float32)).astype(jnp.bfloat16)
    return np.stack([high, low])


def sine_matrix(depth):
    k = np.arange(1, depth + 1)
    return math.sqrt(2.0 / (depth + 1)) * np.sin(np.outer(k, k) * math.pi / (depth + 1))


def decay_tables(depth, y_cells, x_cells, block):
    k1 = y_cells // lanes
    ky = np.arange(k1)[:, None] + k1 * np.arange(lanes)[None, :]
    ez = 2.0 - 2.0 * np.cos(np.arange(1, depth + 1) * math.pi / (depth + 1))
    ey = 2.0 - 2.0 * np.cos(ky.reshape(-1) * 2.0 * math.pi / y_cells)
    lam = screening + ez[:, None] + ey[None, :]
    root = np.sqrt(lam + 0.25 * lam * lam)
    r = 1.0 / (1.0 + 0.5 * lam + root)
    return np.stack([r, 0.5 / root, r**block, 1.0 / (1.0 - r**x_cells)]).astype(np.float32)


def face(near, far, gain):
    return (far - near) + gain * (near + far)


def split_dot(rows, table_ref, pair, contract):
    count = rows.shape[0]
    high = rows.astype(jnp.bfloat16)
    low = (rows - high.astype(jnp.float32)).astype(jnp.bfloat16)

    def product(a, b):
        dims = (((1,), (contract,)), ((), ()))
        return lax.dot_general(a, b, dims, preferred_element_type=jnp.float32)

    main = product(jnp.concatenate([low, high], axis=0), table_ref[0, pair])
    return (product(high, table_ref[1, pair]) + main[:count]) + main[count:]


def halves(value):
    return value[:, :lanes], value[:, lanes:]


def to_modes(rhs, table_ref):
    f = [rhs[:, a * lanes : (a + 1) * lanes] for a in range(8)]
    s = [f[a] + f[a + 4] for a in range(4)]
    d = [f[a] - f[a + 4] for a in range(4)]
    u = diagonal * (d[1] - d[3])
    v = diagonal * (d[1] + d[3])
    even, odd = s[0] + s[2], s[1] + s[3]
    inputs = [
        (even + odd, even - odd),
        (d[0] + u, -(d[2] + v)),
        (s[0] - s[2], s[3] - s[1]),
        (d[0] - u, d[2] - v),
    ]
    blocks = [None] * 8
    for pair, columns in enumerate(inputs):
        out = split_dot(jnp.concatenate(columns, axis=1), table_ref, pair, 0)
        blocks[pair], blocks[8 - pair if pair else 4] = halves(out)
    return blocks


def from_modes(blocks, table_ref):
    outs = []
    for pair in range(4):
        columns = jnp.concatenate([blocks[pair], blocks[8 - pair if pair else 4]], axis=1)
        outs.append(halves(split_dot(columns, table_ref, pair, 1)))
    (p0, p4), (c1, q1), (c2, q2), (c3, q3) = outs
    even, odd = p0 + p4, p0 - p4
    m = diagonal * (c1 - c3)
    n = diagonal * (q1 + q3)
    both, other = c1 + c3, q1 - q3
    return [
        (even + c2) + both,
        (odd - q2) + (m - n),
        (even - c2) - other,
        (odd + q2) - (m + n),
        (even + c2) - both,
        (odd - q2) - (m - n),
        (even - c2) + other,
        (odd + q2) + (m + n),
    ]


def far_layer(n_z):
    return lax.axis_index("gz") % 2 * (n_z - 1)


def far_row(rows):
    return lax.axis_index("xy") % 2 * (rows - 1)


def pack_kernel(
    conc_hbm, pot_hbm, z_far_ref, z_near_ref, x_near_ref, x_far_ref, sems
):
    n_section, n_species, depth, rows, _ = conc_hbm.shape
    z_far = far_layer(depth)
    x_far = far_row(rows)
    copies = []
    for q, (z, ref) in enumerate(((z_far, z_far_ref), (depth - 1 - z_far, z_near_ref))):
        for j in range(n_section):
            pair = [
                pltpu.make_async_copy(
                    conc_hbm.at[j, :, z], ref.at[j, 0:n_species], sems.at[q, j, 0]
                ),
                pltpu.make_async_copy(pot_hbm.at[j, z], ref.at[j, n_species], sems.at[q, j, 1]),
            ]
            for copy in pair:
                copy.start()
            copies.extend(pair)
    for copy in copies:
        copy.wait()
    for x, out_ref in ((x_far, x_far_ref), (rows - 1 - x_far, x_near_ref)):
        for j in range(n_section):
            for q, ref in enumerate((z_far_ref, z_near_ref)):
                for s in range(n_species + 1):
                    to = edge_row(n_section, n_species, depth, j, s, q)
                    out_ref[to : to + 1, :] = ref[j, s, pl.ds(x, 1), :]


def edge_row(n_section, n_species, depth, j, s, q):
    if s < n_species:
        return (j * n_species + s) * depth + q
    return (n_section * n_species + j) * depth + q


def inner_kernel(
    coef_ref, inv_ref, half_ref, prev_ref, z_far_ref, z_near_ref, decay_hbm,
    out_ref, decay_ref, own_ref, sem,
):
    n_section, n_species, depth, rows, y_cells = out_ref.shape
    column = pl.ds(pl.multiple_of(lax.axis_index("gz") * lanes, lanes), lanes)
    decay_copy = pltpu.make_async_copy(decay_hbm.at[:, :, column], decay_ref, sem)
    decay_copy.start()
    row = lax.broadcasted_iota(jnp.int32, (rows, y_cells), 0)
    layers = (z_far_ref, z_near_ref)
    z_far = far_layer(depth)

    def species(s, carry):
        half = half_ref[s]
        totals = []
        for j in range(n_section):
            planes = []
            for ref in layers:
                c = ref[j, s]
                p = ref[j, n_species]
                low = face(pltpu.roll(c, 1, 0), c, half * (p - pltpu.roll(p, 1, 0)))
                low = jnp.where(row == 0, 0.0, low)
                c_next = pltpu.roll(c, y_cells - 1, 1)
                p_next = pltpu.roll(p, y_cells - 1, 1)
                ahead = face(c, c_next, half * (p_next - p))
                planes.append(
                    (pltpu.roll(low, rows - 1, 0) - low) + (ahead - pltpu.roll(ahead, 1, 1))
                )
            step = half * (z_near_ref[j, n_species] - z_far_ref[j, n_species])
            between = face(z_far_ref[j, s], z_near_ref[j, s], step)
            totals.append((planes[0] + between, planes[1] - between))
        for q, z in enumerate((z_far, depth - 1 - z_far)):
            prev = prev_ref[s, z]
            for i in range(n_section):
                c = layers[q][i, s]
                update = inv_ref[i * n_species + s] * (prev - c)
                for j in range(n_section):
                    update = update + coef_ref[(i * n_section + j) * n_species + s] * totals[j][q]
                out_ref[i, s, q] = c + update
        return carry

    lax.fori_loop(0, n_species, species, 0)
    decay_copy.wait()
    index = lax.axis_index("xy")
    solver = index // ring * group + index % group
    own_ref[0:1, :] = decay_ref[2, pl.ds(solver, 1), :]
    own_ref[1:2, :] = decay_ref[3, pl.ds(solver, 1), :]


def outer_kernel(
    coef_ref, half_ref, part_ref, z_far_ref, z_near_ref, z_far_got, z_near_got,
    x_near_sent, x_near_got, x_far_sent, x_far_got, table_ref,
    out_hbm, modes_ref, out_ref, rhs_ref, edge_ref, sems,
):
    n_section, n_species, depth, rows, y_cells = part_ref.shape
    planes = n_species * depth
    kind = lax.broadcasted_iota(jnp.int32, (planes, y_cells), 0) // depth

    def by_species(ref, base):
        value = jnp.full((planes, y_cells), ref[base], jnp.float32)
        for s in range(1, n_species):
            value = jnp.where(kind == s, ref[base + s], value)
        return value

    half_rows = by_species(half_ref, 0)
    sides = ((x_near_sent, x_near_got), (x_far_sent, x_far_got))
    for side, (near, far) in enumerate(sides):
        faces = []
        for j in range(n_section):
            base = n_section * planes + j * depth
            step = far[base : base + depth, :] - near[base : base + depth, :]
            step = jnp.concatenate([step] * n_species, axis=0)
            at = slice(j * planes, (j + 1) * planes)
            faces.append(face(near[at, :], far[at, :], half_rows * step))
        for i in range(n_section):
            update = by_species(coef_ref, i * n_section * n_species) * faces[0]
            for j in range(1, n_section):
                update = update + by_species(coef_ref, (i * n_section + j) * n_species) * faces[j]
            edge_ref[side, i * planes : (i + 1) * planes, :] = update

    pairs = ((z_far_ref, z_far_got), (z_near_ref, z_near_got))
    for i in range(n_section):
        for q in range(depth):
            rhs_ref[i, q] = screening * pairs[q][0][i, n_species]
    row = lax.broadcasted_iota(jnp.int32, (rows, y_cells), 0)
    z_far = far_layer(depth)
    x_far = far_row(rows)
    at_x = (row == rows - 1 - x_far, row == x_far)

    def store(s, q):
        z = z_far if q == 0 else depth - 1 - z_far
        return pltpu.make_async_copy(out_ref.at[:, s, q], out_hbm.at[:, s, z], sems.at[s, q])

    def species(s, carry):
        half = half_ref[s]
        for q, (own, got) in enumerate(pairs):
            faces = []
            for j in range(n_section):
                step = got[j, n_species] - own[j, n_species]
                faces.append(face(own[j, s], got[j, s], half * step))
            for i in range(n_section):
                at = pl.ds(i * planes + s * depth + q, 1)
                update = part_ref[i, s, q]
                for side in range(2):
                    update = update + jnp.where(at_x[side], edge_ref[side, at, :], 0.0)
                for j in range(n_section):
                    update = update + coef_ref[(i * n_section + j) * n_species + s] * faces[j]
                out_ref[i, s, q] = update
                rhs_ref[i, q] += (2.0 * half) * update
            store(s, q).start()
        return carry

    lax.fori_loop(0, n_species, species, 0)
    rhs = rhs_ref[...].reshape(n_section * depth * rows, y_cells)
    for g, block in enumerate(to_modes(rhs, table_ref)):
        modes_ref[g] = block
    for s in range(n_species):
        for q in range(depth):
            store(s, q).wait()


def layer_of(z, n_z):
    g = z // n_z
    return g, int(z % n_z != g % 2 * (n_z - 1))


def sine_rows(planes, table):
    depth = len(planes)
    half = depth // 2
    even = [planes[z] + planes[depth - 1 - z] for z in range(half)]
    odd = [planes[z] - planes[depth - 1 - z] for z in range(half)]
    out = []
    for k in range(depth):
        source = even if k % 2 == 0 else odd
        total = source[0] * float(table[k, 0])
        for z in range(1, half):
            total = total + source[z] * float(table[k, z])
        out.append(total)
    return out


def sine_rows_back(planes, table):
    depth = len(planes)
    out = [None] * depth
    for z in range(depth // 2):
        parts = []
        for parity in range(2):
            total = planes[parity] * float(table[parity, z])
            for k in range(parity + 2, depth, 2):
                total = total + planes[k] * float(table[k, z])
            parts.append(total)
        out[z] = parts[0] + parts[1]
        out[depth - 1 - z] = parts[0] - parts[1]
    return out


def sum_kernel(table, decay_ref, modes_ref, hat_ref, sums_ref, rows_ref):
    n_gz, n_section, n_z, rows, _ = modes_ref.shape
    depth = n_gz * n_z
    r = decay_ref[0]
    where = [layer_of(z, n_z) for z in range(depth)]
    for i in range(n_section):
        planes = [modes_ref[g, i, q] for g, q in where]
        for k, plane in enumerate(sine_rows(planes, table)):
            rows_ref[i, pl.ds(k * rows, rows), :] = plane
        for x in range(rows):
            hat_ref[i, x] = rows_ref[i, pl.ds(x, depth, stride=rows), :]
        ahead = hat_ref[i, 0]
        back = hat_ref[i, rows - 1]
        for x in range(1, rows):
            ahead = ahead * r + hat_ref[i, x]
            back = back * r + hat_ref[i, rows - 1 - x]
        for side, value in enumerate((ahead, back)):
            at = side * n_section + i
            for y in range(depth // group):
                four = value[y * group : (y + 1) * group]
                for copy in range(ring // group):
                    first = (y * ring + copy * group) * 2 * n_section + at
                    sums_ref[pl.ds(first, group, stride=2 * n_section), :] = four


def ring_kernel(n_section, own_ref, sums_ref, out_ref, all_ref):
    per = 2 * n_section
    n_xy = sums_ref.shape[0] // per
    rho = jnp.broadcast_to(own_ref[0:1, :], (n_section, lanes))
    scale = own_ref[1:2, :]

    def ahead_sum(d):
        return sums_ref[d * per : d * per + n_section, :]

    def back_sum(d):
        return sums_ref[d * per + n_section : (d + 1) * per, :]

    ahead = ahead_sum(0)
    back = back_sum(n_xy - 1)
    for d in range(1, n_xy):
        ahead = ahead * rho + ahead_sum(d)
        back = back * rho + back_sum(n_xy - 1 - d)
    ahead = ahead * scale
    back = back * scale
    for d in range(n_xy):
        e = n_xy - 1 - d
        all_ref[d * per : d * per + n_section, :] = ahead
        all_ref[e * per + n_section : (e + 1) * per, :] = back
        ahead = ahead * rho + ahead_sum(d)
        back = back * rho + back_sum(e)
    mine = lax.axis_index("xy") % ring // group
    span = group * per
    for y in range(n_xy // ring):
        first = pl.multiple_of(y * ring * per + mine * span, 8)
        out_ref[y * span : (y + 1) * span, :] = all_ref[pl.ds(first, span), :]


def solve_kernel(table, decay_ref, hat_ref, enter_ref, out_ref, work_ref, rows_ref):
    n_gz, n_section, n_z, rows, _ = out_ref.shape
    depth = n_gz * n_z
    r = decay_ref[0]
    inverse = decay_ref[1]
    where = [layer_of(z, n_z) for z in range(depth)]
    for i in range(n_section):
        value = enter_ref[pl.ds(i, depth, stride=2 * n_section), :]
        for x in range(rows):
            source = hat_ref[i, x]
            work_ref[x] = value * r
            value = value * r + source
        value = enter_ref[pl.ds(n_section + i, depth, stride=2 * n_section), :]
        for x in range(rows - 1, -1, -1):
            value = value * r + hat_ref[i, x]
            rows_ref[i, pl.ds(x, depth, stride=rows), :] = (work_ref[x] + value) * inverse
        planes = [rows_ref[i, pl.ds(k * rows, rows), :] for k in range(depth)]
        for (g, q), plane in zip(where, sine_rows_back(planes, table)):
            out_ref[g, i, q] = plane


def final_kernel(solved_ref, table_ref, out_ref):
    n_gz, n_section, n_z, rows, _ = solved_ref.shape
    z_far = far_layer(n_z)
    blocks = [solved_ref[g].reshape(n_section * n_z * rows, lanes) for g in range(n_gz)]
    for a, block in enumerate(from_modes(blocks, table_ref)):
        block = block.reshape(n_section, n_z, rows, lanes)
        for i in range(n_section):
            for q, z in enumerate((z_far, n_z - 1 - z_far)):
                out_ref[i, z, :, a * lanes : (a + 1) * lanes] = block[i, q]


def on_device(conc_prev, conc_section, potential, diffusivity, charges):
    n_xy = lax.axis_size("xy")
    n_gz = lax.axis_size("gz")
    n_section, n_species, n_z, rows, y_cells = conc_section.shape
    depth = n_z * n_gz
    x_cells = rows * n_xy
    f32 = jnp.float32
    vmem = pl.BlockSpec(memory_space=pltpu.VMEM)
    smem = pl.BlockSpec(memory_space=pltpu.SMEM)
    hbm = pl.BlockSpec(memory_space=pltpu.HBM)

    def params(mib):
        return pltpu.CompilerParams(vmem_limit_bytes=mib * 1024 * 1024)

    table = jnp.asarray(hartley_tables(y_cells))
    sine = sine_matrix(depth)
    decay = jnp.asarray(decay_tables(depth, y_cells, x_cells, rows))

    layers = jax.ShapeDtypeStruct((n_section, n_species + 1, rows, y_cells), f32)
    edges = jax.ShapeDtypeStruct((n_section * n_z * (n_species + 1), y_cells), f32)
    z_far_out, z_near_out, x_near_out, x_far_out = pl.pallas_call(
        pack_kernel,
        out_shape=(layers, layers, edges, edges),
        in_specs=[hbm] * 2,
        out_specs=(vmem,) * 4,
        scratch_shapes=[pltpu.SemaphoreType.DMA((n_z, n_section, 2))],
        compiler_params=params(50),
        name="pack",
    )(conc_section, potential)

    def swap(value, axis, pairs):
        return lax.ppermute(value, axis, pairs + [(j, i) for i, j in pairs])

    z_far_in = swap(z_far_out, "gz", [(i, i + 1) for i in range(1, n_gz - 1, 2)])
    z_near_in = swap(z_near_out, "gz", [(i, i + 1) for i in range(0, n_gz, 2)])
    x_near_in = swap(x_near_out, "xy", [(i, i + 1) for i in range(0, n_xy, 2)])
    x_far_in = swap(x_far_out, "xy", [(i, (i + 1) % n_xy) for i in range(1, n_xy, 2)])

    butcher = np.asarray(radau_matrix(), np.float32)
    scale_row = 1.0 / (
        1.0 + 6.0 * step_size * np.diag(butcher)[:, None] * diffusivity[None, :]
    )
    coef = (step_size * butcher)[:, :, None] * (diffusivity[None, :] * scale_row)[:, None, :]
    half = 0.5 * charges.astype(f32)
    coef = coef.reshape(-1)

    planes = (n_section, n_species, n_z, rows, y_cells)
    part, decay_here, own = pl.pallas_call(
        inner_kernel,
        out_shape=(
            jax.ShapeDtypeStruct(planes, f32),
            jax.ShapeDtypeStruct((decay.shape[0], depth, lanes), f32),
            jax.ShapeDtypeStruct((2, lanes), f32),
        ),
        in_specs=[smem] * 3 + [vmem] * 3 + [hbm],
        out_specs=(vmem, vmem, vmem),
        scratch_shapes=[pltpu.SemaphoreType.DMA(())],
        compiler_params=params(24),
        cost_estimate=pl.CostEstimate(flops=20_000_000, bytes_accessed=4_500_000, transcendentals=0),
        name="inner_faces",
    )(coef, scale_row.reshape(-1), half, conc_prev, z_far_out, z_near_out, decay)

    conc_new, modes = pl.pallas_call(
        outer_kernel,
        out_shape=(
            jax.ShapeDtypeStruct(conc_section.shape, f32),
            jax.ShapeDtypeStruct((n_gz, n_section * n_z * rows, lanes), f32),
        ),
        in_specs=[smem] * 2 + [vmem] * 10,
        out_specs=(hbm, vmem),
        scratch_shapes=[
            pltpu.VMEM(planes, f32),
            pltpu.VMEM((n_section, n_z, rows, y_cells), f32),
            pltpu.VMEM((2, n_section * n_species * n_z, y_cells), f32),
            pltpu.SemaphoreType.DMA((n_species, n_z)),
        ],
        compiler_params=params(24),
        name="outer_faces",
    )(
        coef, half, part, z_far_out, z_near_out, z_far_in, z_near_in,
        x_near_out, x_near_in, x_far_out, x_far_in, table,
    )

    columns = lax.all_to_all(modes, "gz", split_axis=0, concat_axis=0, tiled=True)
    columns = columns.reshape(n_gz, n_section, n_z, rows, lanes)

    n_rows = 2 * n_section * n_xy
    hat, sums = pl.pallas_call(
        functools.partial(sum_kernel, sine),
        out_shape=(
            jax.ShapeDtypeStruct((n_section, rows, depth, lanes), f32),
            jax.ShapeDtypeStruct((n_rows, lanes), f32),
        ),
        in_specs=[vmem] * 2,
        out_specs=(vmem, vmem),
        scratch_shapes=[pltpu.VMEM((n_section, depth * rows, lanes), f32)],
        compiler_params=params(12),
        name="block_sums",
    )(decay_here, columns)

    sums = sums.reshape(n_xy, n_section, 2, lanes)
    gathered = lax.all_to_all(sums, "xy", split_axis=0, concat_axis=0, tiled=True)
    gathered = gathered.reshape(n_rows, lanes)
    entering = pl.pallas_call(
        functools.partial(ring_kernel, n_section),
        out_shape=jax.ShapeDtypeStruct((2 * n_section * depth, lanes), f32),
        in_specs=[vmem] * 2,
        out_specs=vmem,
        scratch_shapes=[pltpu.VMEM((n_rows, lanes), f32)],
        compiler_params=params(12),
        name="ring",
    )(own, gathered)
    sharers = [
        [y * ring + first + z for y in range(n_xy // ring) for z in range(group)]
        for first in range(0, ring, group)
    ]
    entering = entering.reshape(depth, n_section, 2, lanes)
    enter = lax.all_to_all(
        entering, "xy", split_axis=0, concat_axis=0, tiled=True, axis_index_groups=sharers
    )
    enter = enter.reshape(2 * n_section * depth, lanes)

    solved = pl.pallas_call(
        functools.partial(solve_kernel, sine),
        out_shape=jax.ShapeDtypeStruct((n_gz, n_section, n_z, rows, lanes), f32),
        in_specs=[vmem] * 3,
        out_specs=vmem,
        scratch_shapes=[
            pltpu.VMEM((rows, depth, lanes), f32),
            pltpu.VMEM((n_section, depth * rows, lanes), f32),
        ],
        compiler_params=params(12),
        name="solve",
    )(decay_here, hat, enter)
    returned = lax.all_to_all(solved, "gz", split_axis=0, concat_axis=0, tiled=True)

    potential_new = pl.pallas_call(
        final_kernel,
        out_shape=jax.ShapeDtypeStruct(potential.shape, f32),
        in_specs=[vmem] * 2,
        out_specs=vmem,
        compiler_params=params(12),
        name="back_to_y",
    )(returned, table)
    return (conc_new, potential_new)


def solution(mesh):
    in_specs = (
        P(None, "gz", "xy", None),
        P(None, None, "gz", "xy", None),
        P(None, "gz", "xy", None),
        P(),
        P(),
    )
    out_specs = (P(None, None, "gz", "xy", None), P(None, "gz", "xy", None))
    return jax.shard_map(
        on_device, mesh=mesh, in_specs=in_specs, out_specs=out_specs, check_vma=False
    )
```

time: 116 us -> 102 us (0.88)
  blocking collectives: 31.8 us -> 62.6 us
  waiting for transfers between devices: 21.8 us -> 0.01 us
  starting transfers between devices: 38.6 us -> 22.8 us
  local copies, waits for them, and re-layouts: 6.08 us -> 2.14 us
  other arithmetic: 3.74 us -> 1.5 us
  Pallas kernels: 12.9 us -> 11.6 us
    all_to_all x1 -> x3, blocking collectives: 17.8 us -> 48.7 us  [the longest x1 23.1 us: on_device(): lax.all_to_all(sums, 'xy', split_axis=0, concat_axis=0, tiled=True)]
    all_to_all x2 -> x0, waiting for transfers between devices: 20 us -> none  [the longest x1 12.7 us: on_device(): lax.all_to_all(sums, 'xy', split_axis=0, concat_axis=0, tiled=True)]
    all_to_all x2 -> x0, starting transfers between devices: 16.6 us -> none  [the longest x1 10.7 us: on_device(): lax.all_to_all(sums, 'xy', split_axis=0, concat_axis=0, tiled=True)]
    concatenate x4 -> x0, other arithmetic: 3.59 us -> none  [the longest x1 1.05 us: on_device(): jnp.concatenate([conc_section[:, :, -1], potential[:, None, -1]], axis=1)]
    ppermute x4, waiting for transfers between devices: 1.79 us -> 0.01 us  [swap(): return lax.ppermute(value, axis, pairs + [(j, i) for i, j in pairs])]
    dynamic_slice x2 -> x0, local copies, waits for them, and re-layouts: 1.55 us -> none  [the longest x1 0.79 us: on_device(): scale_here = lax.dynamic_slice_in_dim(decay_here[3], kz_here, 1, 0)]
    squeeze x1 -> x0, local copies, waits for them, and re-layouts: 1.48 us -> none  [on_device(): conc_section[:, :, 0]]
    slice x2 -> x0, local copies, waits for them, and re-layouts: 1.21 us -> none  [the longest x1 1.05 us: on_device(): potential[:, None, 0]]
  transfers between devices with their start and end apart: 6 -> 4, of which waited for: 3 -> 0; matrix products, arithmetic and copies ran while one was open for 4% -> 2% of each run, Pallas kernels for 4% -> 3%
where the time goes in v1:
time: 102 us; the launch traced here: 101 us
  blocking collectives  62.6 us (61%)
  starting transfers between devices  22.8 us (22%)
  Pallas kernels  11.6 us (11%)
  local copies, waits for them, and re-layouts  2.14 us (2%)
  other arithmetic  1.5 us (1%)
    all_to_all x1, blocking collectives, on_device(): lax.all_to_all(sums, 'xy', split_axis=0, concat_axis=0, tiled=True)  23.1 us
    ppermute x4, starting transfers between devices, swap(): return lax.ppermute(value, axis, pairs + [(j, i) for i, j in pairs])  22.8 us
    all_to_all x1, blocking collectives, on_device(): lax.all_to_all(solved, 'gz', split_axis=0, concat_axis=0, tiled=True)  13.9 us
    all_to_all x1, blocking collectives, on_device(): lax.all_to_all(modes, 'gz', split_axis=0, concat_axis=0, tiled=True)  12.9 us
    all_to_all x1, blocking collectives, on_device(): lax.all_to_all(entering, 'xy', split_axis=0, concat_axis=0, tiled=True, a...  12.7 us
    pallas_call x1, Pallas kernels, on_device(): pl.pallas_call(outer_kernel, out_shape=(jax.ShapeDtypeStruct(conc_section...  3.62 us
    pallas_call x1, Pallas kernels, on_device(): pl.pallas_call(inner_kernel, out_shape=(jax.ShapeDtypeStruct(planes, f32)...  3.34 us
    pallas_call x1, Pallas kernels, on_device(): pl.pallas_call(pack_kernel, out_shape=(layers, layers, edges, edges), in_...  2.4 us
  transfers between devices with their start and end apart: 4, of which 0 were waited for; matrix products, arithmetic and copies ran while one was open for 2% of the time, Pallas kernels for 3%

profile of v1, /device:TPU:1, one launch (start us, length us, event | category | flops | bytes accessed | tf_op | source)
XLA Modules:
  0.0 101.4 jit_solution(752199284400997586)
XLA Ops:
  0.6 0.0 copy-start.5
  0.7 1.0 copy-done.2
  1.6 2.4 %pack.1 = (f32[3,5,16,1024]{3,2,1,0:T(8,128)S(1)}, f32[3,5,16,1024]{3,2,1,0:T(8,128)S(1)}, f32[30,1024]{1,0:T(8,128)}, f32[30,1024]{1,0:T(8,128)}) custom-call(f32[3,4,2,16,1024]{4,3,2,1,0:T(8,128)} %conc_hbm.1, f32[3,2,16,1024]{3,2,1,0:T(8,128)S(1)} %copy-done.2), custom_call_target="tpu_custom_call" | custom-call | tf_op jit(solution)/shard_map/pack/pallas_call | solution.py:429
  4.1 0.0 copy-start
  4.1 4.6 %collective-permute-start = (f32[3,5,16,1024]{3,2,1,0:T(8,128)S(1)}, f32[3,5,16,1024]{3,2,1,0:T(8,128)}, u32[]{:S(2)}, u32[]{:S(2)}) collective-permute-start(f32[3,5,16,1024]{3,2,1,0:T(8,128)S(1)} %get-tuple-element.13.z_far_ref), channel_id=1, source_target_pairs={{1,2},{3,4},{5,6},{2,1},{4,3},{6,5},{9,10},{11,12},{13,14},{10,9},... | collective-permute-start | bytes 2949128 | tf_op jit(solution)/shard_map/ppermute | solution.py:440
  8.7 5.9 %collective-permute-start.1 = (f32[3,5,16,1024]{3,2,1,0:T(8,128)S(1)}, f32[3,5,16,1024]{3,2,1,0:T(8,128)}, u32[]{:S(2)}, u32[]{:S(2)}) collective-permute-start(f32[3,5,16,1024]{3,2,1,0:T(8,128)S(1)} %get-tuple-element.14.z_near_ref), channel_id=1, source_target_pairs={{0,1},{2,3},{4,5},{6,7},{1,0},{3,2},{5,4},{7,6},{8,9},{10,11},{12,... | collective-permute-start | bytes 2949128 | tf_op jit(solution)/shard_map/ppermute | solution.py:440
  14.6 1.9 %collective-permute-start.2 = (f32[30,1024]{1,0:T(8,128)}, f32[30,1024]{1,0:T(8,128)}, u32[]{:S(2)}, u32[]{:S(2)}) collective-permute-start(f32[30,1024]{1,0:T(8,128)} %get-tuple-element.16.x_near_sent), channel_id=1, source_target_pairs={{0,8},{16,24},{32,40},{48,56},{64,72},{80,88},{96,104},{112,120},{... | collective-permute-start | bytes 368648 | tf_op jit(solution)/shard_map/ppermute | solution.py:440
  16.5 10.3 %collective-permute-start.3 = (f32[30,1024]{1,0:T(8,128)}, f32[30,1024]{1,0:T(8,128)}, u32[]{:S(2)}, u32[]{:S(2)}) collective-permute-start(f32[30,1024]{1,0:T(8,128)} %get-tuple-element.17.x_far_sent), channel_id=1, source_target_pairs={{8,16},{24,32},{40,48},{56,64},{72,80},{88,96},{104,112},{120,128}... | collective-permute-start | bytes 368648 | tf_op jit(solution)/shard_map/ppermute | solution.py:440
  26.9 0.1 add_divide_fusion
  27.0 0.1 div.12.inv_ref
  27.1 0.8 broadcast_multiply_fusion
  27.8 0.1 mul.62.coef_ref
  27.9 0.7 convert_multiply_fusion.half_ref
  28.6 0.9 copy-done.3
  29.5 3.3 %inner_faces.1 = (f32[3,4,2,16,1024]{4,3,2,1,0:T(8,128)S(1)}, f32[4,16,128]{2,1,0:T(8,128)S(1)}, f32[2,128]{1,0:T(2,128)S(1)}) custom-call(f32[36]{0:T(128)S(1)} %mul.62.coef_ref, f32[12]{0:T(128)S(1)} %div.12.inv_ref, f32[4]{0:T(128)S(1)} %convert_multiply_fusion.half_ref, f32[4,2,16,1024]{3,2,1,0:T(8,128)S(1)} %copy-done.1, ...), custom_call_target="tpu_custom_call" | custom-call | flops 20000000 | bytes 4500000 | tf_op jit(solution)/shard_map/inner_faces/pallas_call | solution.py:456
  32.9 3.6 %outer_faces.1 = (f32[3,4,2,16,1024]{4,3,2,1,0:T(8,128)}, f32[8,96,128]{2,1,0:T(8,128)S(1)}) custom-call(f32[36]{0:T(128)S(1)} %mul.62.coef_ref, f32[4]{0:T(128)S(1)} %convert_multiply_fusion.half_ref, f32[3,4,2,16,1024]{4,3,2,1,0:T(8,128)S(1)} %get-tuple-element.15.part_ref, f32[3,5,16,1024]{3,2,1,0:T(8,128)S(1)} %get-tuple-element.13.z_far_ref, ...), custom_call_target="tpu_custom_call" | custom-call | tf_op jit(solution)/shard_map/outer_faces/pallas_call | solution.py:471
  36.6 12.9 %all_to_all.20 = f32[8,96,128]{2,1,0:T(8,128)S(1)} all-to-all(f32[8,96,128]{2,1,0:T(8,128)S(1)} %get-tuple-element.20), channel_id=1, replica_groups=mesh['xy'=64,'gz'=8] {'gz'}, dimensions={0} | all-to-all | bytes 786432 | tf_op jit(solution)/shard_map/all_to_all | solution.py:492
  49.5 0.4 block_sums.1
  49.9 23.1 %all_to_all.21 = f32[64,3,2,128]{3,2,1,0:T(2,128)S(1)} all-to-all(f32[64,3,2,128]{3,2,1,0:T(2,128)S(1)} %bitcast.7), channel_id=1, replica_groups=mesh['xy'=64,'gz'=8] {'xy'}, dimensions={0} | all-to-all | bytes 393216 | tf_op jit(solution)/shard_map/all_to_all | solution.py:510
  73.0 0.3 ring.1
  73.2 12.7 %all_to_all.22 = f32[16,3,2,128]{3,2,1,0:T(2,128)S(1)} all-to-all(f32[16,3,2,128]{3,2,1,0:T(2,128)S(1)} %bitcast.8), channel_id=1, replica_groups={{0,8,16,24,128,136,144,152,256,264,272,280,384,392,400,408},{32,40,48,5..., dimensions={0} | all-to-all | bytes 98304 | tf_op jit(solution)/shard_map/all_to_all | solution.py:526
  85.9 0.4 solve.1
  86.3 13.9 %all_to_all.23.solved_ref = f32[8,3,2,16,128]{4,3,2,1,0:T(8,128)S(1)} all-to-all(f32[8,3,2,16,128]{4,3,2,1,0:T(8,128)S(1)} %solve.1), channel_id=1, replica_groups=mesh['xy'=64,'gz'=8] {'gz'}, dimensions={0} | all-to-all | bytes 786432 | tf_op jit(solution)/shard_map/all_to_all | solution.py:543
  100.2 1.2 %back_to_y.1 = f32[3,2,16,1024]{3,2,1,0:T(8,128)} custom-call(f32[8,3,2,16,128]{4,3,2,1,0:T(8,128)S(1)} %all_to_all.23.solved_ref, bf16[2,4,256,256]{3,2,1,0:T(8,128)(2,1)S(1)} %copy-done), custom_call_target="tpu_custom_call" | custom-call | tf_op jit(solution)/shard_map/back_to_y/pallas_call | solution.py:545
  (12 shorter events, 0.0 us)
Async XLA Ops:
  0.6 26.3 %copy-start.5 = (f32[3]{0:T(128)S(1)}, f32[3]{0:T(128)}, u32[]{:S(2)}) copy-start(f32[3]{0:T(128)} %constant.20) | copy-start | bytes 40
  0.6 1.0 copy-start.2
  1.6 25.2 %copy-start.4 = (f32[4]{0:T(128)S(1)}, f32[4]{0:T(128)}, u32[]{:S(2)}) copy-start(f32[4]{0:T(128)} %param.12) | copy-start | bytes 52
  1.6 26.9 %copy-start.1 = (f32[4,2,16,1024]{3,2,1,0:T(8,128)S(1)}, f32[4,2,16,1024]{3,2,1,0:T(8,128)}, u32[]{:S(2)}) copy-start(f32[4,2,16,1024]{3,2,1,0:T(8,128)} %prev_ref.1) | copy-start | bytes 1572868
  4.1 28.9 %copy-start = (bf16[2,4,256,256]{3,2,1,0:T(8,128)(2,1)S(1)}, bf16[2,4,256,256]{3,2,1,0:T(8,128)(2,1)}, u32[]{:S(2)}) copy-start(bf16[2,4,256,256]{3,2,1,0:T(8,128)(2,1)} %constant.12.clone.table_ref) | copy-start | bytes 3145732
  4.1 28.8 %collective-permute-start = (f32[3,5,16,1024]{3,2,1,0:T(8,128)S(1)}, f32[3,5,16,1024]{3,2,1,0:T(8,128)}, u32[]{:S(2)}, u32[]{:S(2)}) collective-permute-start(f32[3,5,16,1024]{3,2,1,0:T(8,128)S(1)} %get-tuple-element.13.z_far_ref), channel_id=1, source_target_pairs={{1,2},{3,4},{5,6},{2,1},{4,3},{6,5},{9,10},{11,12},{13,14},{10,9},... | collective-permute-start | bytes 2949128 | tf_op jit(solution)/shard_map/ppermute | solution.py:440
  8.7 24.2 %collective-permute-start.1 = (f32[3,5,16,1024]{3,2,1,0:T(8,128)S(1)}, f32[3,5,16,1024]{3,2,1,0:T(8,128)}, u32[]{:S(2)}, u32[]{:S(2)}) collective-permute-start(f32[3,5,16,1024]{3,2,1,0:T(8,128)S(1)} %get-tuple-element.14.z_near_ref), channel_id=1, source_target_pairs={{0,1},{2,3},{4,5},{6,7},{1,0},{3,2},{5,4},{7,6},{8,9},{10,11},{12,... | collective-permute-start | bytes 2949128 | tf_op jit(solution)/shard_map/ppermute | solution.py:440
  14.6 18.3 %collective-permute-start.2 = (f32[30,1024]{1,0:T(8,128)}, f32[30,1024]{1,0:T(8,128)}, u32[]{:S(2)}, u32[]{:S(2)}) collective-permute-start(f32[30,1024]{1,0:T(8,128)} %get-tuple-element.16.x_near_sent), channel_id=1, source_target_pairs={{0,8},{16,24},{32,40},{48,56},{64,72},{80,88},{96,104},{112,120},{... | collective-permute-start | bytes 368648 | tf_op jit(solution)/shard_map/ppermute | solution.py:440
  16.5 16.3 %collective-permute-start.3 = (f32[30,1024]{1,0:T(8,128)}, f32[30,1024]{1,0:T(8,128)}, u32[]{:S(2)}, u32[]{:S(2)}) collective-permute-start(f32[30,1024]{1,0:T(8,128)} %get-tuple-element.17.x_far_sent), channel_id=1, source_target_pairs={{8,16},{24,32},{40,48},{56,64},{72,80},{88,96},{104,112},{120,128}... | collective-permute-start | bytes 368648 | tf_op jit(solution)/shard_map/ppermute | solution.py:440
  28.6 1.0 copy-start.3

commit v2 on v1

--- a/solution.py
+++ b/solution.py
@@ -45,15 +45,18 @@
     return math.sqrt(2.0 / (depth + 1)) * np.sin(np.outer(k, k) * math.pi / (depth + 1))
 
 
-def decay_tables(depth, y_cells, x_cells, block):
+def wave_table(depth, y_cells):
     k1 = y_cells // lanes
     ky = np.arange(k1)[:, None] + k1 * np.arange(lanes)[None, :]
+    ey = 2.0 - 2.0 * np.cos(ky * 2.0 * math.pi / y_cells)
     ez = 2.0 - 2.0 * np.cos(np.arange(1, depth + 1) * math.pi / (depth + 1))
-    ey = 2.0 - 2.0 * np.cos(ky.reshape(-1) * 2.0 * math.pi / y_cells)
-    lam = screening + ez[:, None] + ey[None, :]
-    root = np.sqrt(lam + 0.25 * lam * lam)
-    r = 1.0 / (1.0 + 0.5 * lam + root)
-    return np.stack([r, 0.5 / root, r**block, 1.0 / (1.0 - r**x_cells)]).astype(np.float32)
+    return np.concatenate([ey, np.broadcast_to(ez[:, None], (depth, lanes))]).astype(np.float32)
+
+
+def power(value, exponent):
+    for _ in range(exponent.bit_length() - 1):
+        value = value * value
+    return value
 
 
 def face(near, far, gain):
@@ -117,6 +120,16 @@
         (even - c2) + other,
         (odd + q2) + (m + n),
     ]
+
+
+def coefficients(diffusivity_ref, s):
+    matrix = radau_matrix()
+    d = diffusivity_ref[s]
+    inverse, coef = [], []
+    for i, row in enumerate(matrix):
+        inverse.append(1.0 / (1.0 + (6.0 * step_size * row[i]) * d))
+        coef.append([(step_size * entry) * d * inverse[i] for entry in row])
+    return inverse, coef
 
 
 def far_layer(n_z):
@@ -162,83 +175,93 @@
 
 
 def inner_kernel(
-    coef_ref, inv_ref, half_ref, prev_ref, z_far_ref, z_near_ref, decay_hbm,
-    out_ref, decay_ref, own_ref, sem,
+    diffusivity_ref, charge_ref, prev_ref, z_far_ref, z_near_ref, wave_ref,
+    out_ref, decay_ref, own_ref, step_ref, between_ref,
 ):
     n_section, n_species, depth, rows, y_cells = out_ref.shape
-    column = pl.ds(pl.multiple_of(lax.axis_index("gz") * lanes, lanes), lanes)
-    decay_copy = pltpu.make_async_copy(decay_hbm.at[:, :, column], decay_ref, sem)
-    decay_copy.start()
     row = lax.broadcasted_iota(jnp.int32, (rows, y_cells), 0)
     layers = (z_far_ref, z_near_ref)
     z_far = far_layer(depth)
+    for j in range(n_section):
+        for q, ref in enumerate(layers):
+            p = ref[j, n_species]
+            step_ref[j, q, 0] = p - pltpu.roll(p, 1, 0)
+            step_ref[j, q, 1] = pltpu.roll(p, y_cells - 1, 1) - p
+        between_ref[j] = z_near_ref[j, n_species] - z_far_ref[j, n_species]
 
     def species(s, carry):
-        half = half_ref[s]
+        half = 0.5 * charge_ref[s].astype(jnp.float32)
+        inverse, coef = coefficients(diffusivity_ref, s)
         totals = []
         for j in range(n_section):
             planes = []
-            for ref in layers:
+            for q, ref in enumerate(layers):
                 c = ref[j, s]
-                p = ref[j, n_species]
-                low = face(pltpu.roll(c, 1, 0), c, half * (p - pltpu.roll(p, 1, 0)))
+                low = face(pltpu.roll(c, 1, 0), c, half * step_ref[j, q, 0])
                 low = jnp.where(row == 0, 0.0, low)
-                c_next = pltpu.roll(c, y_cells - 1, 1)
-                p_next = pltpu.roll(p, y_cells - 1, 1)
-                ahead = face(c, c_next, half * (p_next - p))
+                ahead = face(c, pltpu.roll(c, y_cells - 1, 1), half * step_ref[j, q, 1])
                 planes.append(
                     (pltpu.roll(low, rows - 1, 0) - low) + (ahead - pltpu.roll(ahead, 1, 1))
                 )
-            step = half * (z_near_ref[j, n_species] - z_far_ref[j, n_species])
-            between = face(z_far_ref[j, s], z_near_ref[j, s], step)
+            between = face(z_far_ref[j, s], z_near_ref[j, s], half * between_ref[j])
             totals.append((planes[0] + between, planes[1] - between))
         for q, z in enumerate((z_far, depth - 1 - z_far)):
             prev = prev_ref[s, z]
             for i in range(n_section):
                 c = layers[q][i, s]
-                update = inv_ref[i * n_species + s] * (prev - c)
+                update = inverse[i] * (prev - c)
                 for j in range(n_section):
-                    update = update + coef_ref[(i * n_section + j) * n_species + s] * totals[j][q]
+                    update = update + coef[i][j] * totals[j][q]
                 out_ref[i, s, q] = c + update
         return carry
 
     lax.fori_loop(0, n_species, species, 0)
-    decay_copy.wait()
+    k1 = wave_ref.shape[0] - decay_ref.shape[1]
+    lam = screening + wave_ref[pl.ds(lax.axis_index("gz"), 1), :] + wave_ref[k1:, :]
+    root = jnp.sqrt(lam + 0.25 * lam * lam)
+    r = 1.0 / (1.0 + 0.5 * lam + root)
+    decay_ref[0] = r
+    decay_ref[1] = 0.5 / root
+    decay_ref[2] = power(r, rows)
     index = lax.axis_index("xy")
     solver = index // ring * group + index % group
-    own_ref[0:1, :] = decay_ref[2, pl.ds(solver, 1), :]
-    own_ref[1:2, :] = decay_ref[3, pl.ds(solver, 1), :]
+    rho = decay_ref[2, pl.ds(solver, 1), :]
+    own_ref[0:1, :] = rho
+    own_ref[1:2, :] = 1.0 / (1.0 - power(rho, lax.axis_size("xy")))
 
 
 def outer_kernel(
-    coef_ref, half_ref, part_ref, z_far_ref, z_near_ref, z_far_got, z_near_got,
-    x_near_sent, x_near_got, x_far_sent, x_far_got, table_ref,
+    diffusivity_ref, charge_ref, part_ref, z_far_ref, z_near_ref, z_far_got,
+    x_far_sent, x_far_got, x_near_sent, x_near_got, z_near_got, table_ref,
     out_hbm, modes_ref, out_ref, rhs_ref, edge_ref, sems,
 ):
     n_section, n_species, depth, rows, y_cells = part_ref.shape
     planes = n_species * depth
     kind = lax.broadcasted_iota(jnp.int32, (planes, y_cells), 0) // depth
-
-    def by_species(ref, base):
-        value = jnp.full((planes, y_cells), ref[base], jnp.float32)
+    by_row = [coefficients(diffusivity_ref, s)[1] for s in range(n_species)]
+
+    def by_species(values):
+        total = jnp.full((planes, y_cells), values[0], jnp.float32)
         for s in range(1, n_species):
-            value = jnp.where(kind == s, ref[base + s], value)
-        return value
-
-    half_rows = by_species(half_ref, 0)
+            total = jnp.where(kind == s, values[s], total)
+        return total
+
+    half_rows = by_species([0.5 * charge_ref[s].astype(jnp.float32) for s in range(n_species)])
     sides = ((x_near_sent, x_near_got), (x_far_sent, x_far_got))
-    for side, (near, far) in enumerate(sides):
-        faces = []
+    faces = []
+    for near, far in sides:
         for j in range(n_section):
             base = n_section * planes + j * depth
             step = far[base : base + depth, :] - near[base : base + depth, :]
             step = jnp.concatenate([step] * n_species, axis=0)
             at = slice(j * planes, (j + 1) * planes)
             faces.append(face(near[at, :], far[at, :], half_rows * step))
-        for i in range(n_section):
-            update = by_species(coef_ref, i * n_section * n_species) * faces[0]
+    for i in range(n_section):
+        weights = [by_species([by_row[s][i][j] for s in range(n_species)]) for j in range(n_section)]
+        for side in range(2):
+            update = weights[0] * faces[side * n_section]
             for j in range(1, n_section):
-                update = update + by_species(coef_ref, (i * n_section + j) * n_species) * faces[j]
+                update = update + weights[j] * faces[side * n_section + j]
             edge_ref[side, i * planes : (i + 1) * planes, :] = update
 
     pairs = ((z_far_ref, z_far_got), (z_near_ref, z_near_got))
@@ -255,7 +278,8 @@
         return pltpu.make_async_copy(out_ref.at[:, s, q], out_hbm.at[:, s, z], sems.at[s, q])
 
     def species(s, carry):
-        half = half_ref[s]
+        half = 0.5 * charge_ref[s].astype(jnp.float32)
+        _, coef = coefficients(diffusivity_ref, s)
         for q, (own, got) in enumerate(pairs):
             faces = []
             for j in range(n_section):
@@ -267,7 +291,7 @@
                 for side in range(2):
                     update = update + jnp.where(at_x[side], edge_ref[side, at, :], 0.0)
                 for j in range(n_section):
-                    update = update + coef_ref[(i * n_section + j) * n_species + s] * faces[j]
+                    update = update + coef[i][j] * faces[j]
                 out_ref[i, s, q] = update
                 rhs_ref[i, q] += (2.0 * half) * update
             store(s, q).start()
@@ -411,7 +435,6 @@
     n_gz = lax.axis_size("gz")
     n_section, n_species, n_z, rows, y_cells = conc_section.shape
     depth = n_z * n_gz
-    x_cells = rows * n_xy
     f32 = jnp.float32
     vmem = pl.BlockSpec(memory_space=pltpu.VMEM)
     smem = pl.BlockSpec(memory_space=pltpu.SMEM)
@@ -422,7 +445,7 @@
 
     table = jnp.asarray(hartley_tables(y_cells))
     sine = sine_matrix(depth)
-    decay = jnp.asarray(decay_tables(depth, y_cells, x_cells, rows))
+    wave = jnp.asarray(wave_table(depth, y_cells))
 
     layers = jax.ShapeDtypeStruct((n_section, n_species + 1, rows, y_cells), f32)
     edges = jax.ShapeDtypeStruct((n_section * n_z * (n_species + 1), y_cells), f32)
@@ -440,33 +463,28 @@
         return lax.ppermute(value, axis, pairs + [(j, i) for i, j in pairs])
 
     z_far_in = swap(z_far_out, "gz", [(i, i + 1) for i in range(1, n_gz - 1, 2)])
+    x_far_in = swap(x_far_out, "xy", [(i, (i + 1) % n_xy) for i in range(1, n_xy, 2)])
+    x_near_in = swap(x_near_out, "xy", [(i, i + 1) for i in range(0, n_xy, 2)])
     z_near_in = swap(z_near_out, "gz", [(i, i + 1) for i in range(0, n_gz, 2)])
-    x_near_in = swap(x_near_out, "xy", [(i, i + 1) for i in range(0, n_xy, 2)])
-    x_far_in = swap(x_far_out, "xy", [(i, (i + 1) % n_xy) for i in range(1, n_xy, 2)])
-
-    butcher = np.asarray(radau_matrix(), np.float32)
-    scale_row = 1.0 / (
-        1.0 + 6.0 * step_size * np.diag(butcher)[:, None] * diffusivity[None, :]
-    )
-    coef = (step_size * butcher)[:, :, None] * (diffusivity[None, :] * scale_row)[:, None, :]
-    half = 0.5 * charges.astype(f32)
-    coef = coef.reshape(-1)
 
     planes = (n_section, n_species, n_z, rows, y_cells)
     part, decay_here, own = pl.pallas_call(
         inner_kernel,
         out_shape=(
             jax.ShapeDtypeStruct(planes, f32),
-            jax.ShapeDtypeStruct((decay.shape[0], depth, lanes), f32),
+            jax.ShapeDtypeStruct((3, depth, lanes), f32),
             jax.ShapeDtypeStruct((2, lanes), f32),
         ),
-        in_specs=[smem] * 3 + [vmem] * 3 + [hbm],
+        in_specs=[smem] * 2 + [vmem] * 4,
         out_specs=(vmem, vmem, vmem),
-        scratch_shapes=[pltpu.SemaphoreType.DMA(())],
+        scratch_shapes=[
+            pltpu.VMEM((n_section, n_z, 2, rows, y_cells), f32),
+            pltpu.VMEM((n_section, rows, y_cells), f32),
+        ],
         compiler_params=params(24),
         cost_estimate=pl.CostEstimate(flops=20_000_000, bytes_accessed=4_500_000, transcendentals=0),
         name="inner_faces",
-    )(coef, scale_row.reshape(-1), half, conc_prev, z_far_out, z_near_out, decay)
+    )(diffusivity, charges, conc_prev, z_far_out, z_near_out, wave)
 
     conc_new, modes = pl.pallas_call(
         outer_kernel,
@@ -485,8 +503,8 @@
         compiler_params=params(24),
         name="outer_faces",
     )(
-        coef, half, part, z_far_out, z_near_out, z_far_in, z_near_in,
-        x_near_out, x_near_in, x_far_out, x_far_in, table,
+        diffusivity, charges, part, z_far_out, z_near_out, z_far_in,
+        x_far_out, x_far_in, x_near_out, x_near_in, z_near_in, table,
     )
 
     columns = lax.all_to_all(modes, "gz", split_axis=0, concat_axis=0, tiled=True)

time: 102 us -> 99 us (0.971)
  Pallas kernels: 11.6 us -> 9.62 us
  other arithmetic: 1.5 us -> 0 us
  blocking collectives: 62.6 us -> 63.9 us
  waiting for transfers between devices: 0.01 us -> 1.27 us
  local copies, waits for them, and re-layouts: 2.14 us -> 1.01 us
    mul x2 -> x0, other arithmetic: 1.42 us -> none  [the longest x1 0.76 us: on_device(): (step_size * butcher)[:, :, None]]
    ppermute x4, waiting for transfers between devices: 0.01 us -> 1.27 us  [swap(): return lax.ppermute(value, axis, pairs + [(j, i) for i, j in pairs])]
  transfers between devices with their start and end apart: 4 -> 4, of which waited for: 0 -> 1; matrix products, arithmetic and copies ran while one was open for 2% -> 0% of each run, Pallas kernels for 3% -> 3%
where the time goes in v2:
time: 99 us; the launch traced here: 98.6 us
  blocking collectives  63.9 us (65%)
  starting transfers between devices  22.1 us (22%)
  Pallas kernels  9.62 us (10%)
  waiting for transfers between devices  1.27 us (1%)
  local copies, waits for them, and re-layouts  1.01 us (1%)
    all_to_all x1, blocking collectives, on_device(): lax.all_to_all(sums, 'xy', split_axis=0, concat_axis=0, tiled=True)  23.8 us
    ppermute x4, starting transfers between devices, swap(): return lax.ppermute(value, axis, pairs + [(j, i) for i, j in pairs])  22.1 us
    all_to_all x1, blocking collectives, on_device(): lax.all_to_all(solved, 'gz', split_axis=0, concat_axis=0, tiled=True)  13.9 us
    all_to_all x1, blocking collectives, on_device(): lax.all_to_all(modes, 'gz', split_axis=0, concat_axis=0, tiled=True)  13.6 us
    all_to_all x1, blocking collectives, on_device(): lax.all_to_all(entering, 'xy', split_axis=0, concat_axis=0, tiled=True, a...  12.7 us
    pallas_call x1, Pallas kernels, on_device(): pl.pallas_call(inner_kernel, out_shape=(jax.ShapeDtypeStruct(planes, f32)...  2.9 us
    pallas_call x1, Pallas kernels, on_device(): pl.pallas_call(outer_kernel, out_shape=(jax.ShapeDtypeStruct(conc_section...  2.66 us
  transfers between devices with their start and end apart: 4, of which 1 were waited for; matrix products, arithmetic and copies ran while one was open for 0% of the time, Pallas kernels for 3%

profile of v2, /device:TPU:1, one launch (start us, length us, event | category | flops | bytes accessed | tf_op | source)
XLA Modules:
  0.0 98.6 jit_solution(8235588508200770470)
XLA Ops:
  0.6 0.0 copy-start.2
  0.6 1.0 %copy-done.2 = f32[3,2,16,1024]{3,2,1,0:T(8,128)S(1)} copy-done((f32[3,2,16,1024]{3,2,1,0:T(8,128)S(1)}, f32[3,2,16,1024]{3,2,1,0:T(8,128)}, u32[]{:S(2)}) %copy-start.2) | copy-done | bytes 393240
  1.6 1.8 %pack.1 = (f32[3,5,16,1024]{3,2,1,0:T(8,128)S(1)}, f32[3,5,16,1024]{3,2,1,0:T(8,128)S(1)}, f32[30,1024]{1,0:T(8,128)S(1)}, f32[30,1024]{1,0:T(8,128)S(1)}) custom-call(f32[3,4,2,16,1024]{4,3,2,1,0:T(8,128)} %conc_hbm.1, f32[3,2,16,1024]{3,2,1,0:T(8,128)S(1)} %copy-done.2), custom_call_target="tpu_custom_call" | custom-call | tf_op jit(solution)/shard_map/pack/pallas_call | solution.py:452
  3.4 0.0 copy-start
  3.4 4.6 %collective-permute-start = (f32[3,5,16,1024]{3,2,1,0:T(8,128)S(1)}, f32[3,5,16,1024]{3,2,1,0:T(8,128)S(1)}, u32[]{:S(2)}, u32[]{:S(2)}) collective-permute-start(f32[3,5,16,1024]{3,2,1,0:T(8,128)S(1)} %get-tuple-element.13.z_far_ref), channel_id=1, source_target_pairs={{1,2},{3,4},{5,6},{2,1},{4,3},{6,5},{9,10},{11,12},{13,14},{10,9},... | collective-permute-start | bytes 2949128 | tf_op jit(solution)/shard_map/ppermute | solution.py:463
  8.1 5.0 %collective-permute-start.3 = (f32[3,5,16,1024]{3,2,1,0:T(8,128)S(1)}, f32[3,5,16,1024]{3,2,1,0:T(8,128)S(1)}, u32[]{:S(2)}, u32[]{:S(2)}) collective-permute-start(f32[3,5,16,1024]{3,2,1,0:T(8,128)S(1)} %get-tuple-element.14.z_near_ref), channel_id=1, source_target_pairs={{0,1},{2,3},{4,5},{6,7},{1,0},{3,2},{5,4},{7,6},{8,9},{10,11},{12,... | collective-permute-start | bytes 2949128 | tf_op jit(solution)/shard_map/ppermute | solution.py:463
  13.1 10.5 %collective-permute-start.1 = (f32[30,1024]{1,0:T(8,128)S(1)}, f32[30,1024]{1,0:T(8,128)S(1)}, u32[]{:S(2)}, u32[]{:S(2)}) collective-permute-start(f32[30,1024]{1,0:T(8,128)S(1)} %get-tuple-element.16.x_far_sent), channel_id=1, source_target_pairs={{8,16},{24,32},{40,48},{56,64},{72,80},{88,96},{104,112},{120,128}... | collective-permute-start | bytes 368648 | tf_op jit(solution)/shard_map/ppermute | solution.py:463
  23.6 1.9 %collective-permute-start.2 = (f32[30,1024]{1,0:T(8,128)S(1)}, f32[30,1024]{1,0:T(8,128)S(1)}, u32[]{:S(2)}, u32[]{:S(2)}) collective-permute-start(f32[30,1024]{1,0:T(8,128)S(1)} %get-tuple-element.17.x_near_sent), channel_id=1, source_target_pairs={{0,8},{16,24},{32,40},{48,56},{64,72},{80,88},{96,104},{112,120},{... | collective-permute-start | bytes 368648 | tf_op jit(solution)/shard_map/ppermute | solution.py:463
  25.5 0.0 copy-done.1
  25.5 0.0 copy-done.3
  25.6 2.9 %inner_faces.1 = (f32[3,4,2,16,1024]{4,3,2,1,0:T(8,128)S(1)}, f32[3,16,128]{2,1,0:T(8,128)S(1)}, f32[2,128]{1,0:T(2,128)S(1)}) custom-call(f32[4]{0:T(128)S(1)} %copy-done.4, s32[4]{0:T(128)S(1)} %copy-done.5, f32[4,2,16,1024]{3,2,1,0:T(8,128)S(1)} %copy-done.1, f32[3,5,16,1024]{3,2,1,0:T(8,128)S(1)} %get-tuple-element.13.z_far_ref, ...), custom_call_target="tpu_custom_call" | custom-call | flops 20000000 | bytes 4500000 | tf_op jit(solution)/shard_map/inner_faces/pallas_call | solution.py:471
  28.5 0.0 collective-permute-done.1.x_far_got
  28.5 1.3 %collective-permute-done.2.x_near_got = f32[30,1024]{1,0:T(8,128)S(1)} collective-permute-done((f32[30,1024]{1,0:T(8,128)S(1)}, f32[30,1024]{1,0:T(8,128)S(1)}, u32[]{:S(2)}, u32[]{:S(2)}) %collective-permute-start.2) | collective-permute-done | bytes 122912 | tf_op jit(solution)/shard_map/ppermute | solution.py:463
  29.7 0.0 collective-permute-done.z_far_got
  29.7 0.0 collective-permute-done.3.z_near_got
  29.7 2.7 %outer_faces.1 = (f32[3,4,2,16,1024]{4,3,2,1,0:T(8,128)}, f32[8,96,128]{2,1,0:T(8,128)S(1)}) custom-call(f32[4]{0:T(128)S(1)} %copy-done.4, s32[4]{0:T(128)S(1)} %copy-done.5, f32[3,4,2,16,1024]{4,3,2,1,0:T(8,128)S(1)} %get-tuple-element.15.part_ref, f32[3,5,16,1024]{3,2,1,0:T(8,128)S(1)} %get-tuple-element.13.z_far_ref, ...), custom_call_target="tpu_custom_call" | custom-call | tf_op jit(solution)/shard_map/outer_faces/pallas_call | solution.py:489
  32.4 13.6 %all_to_all.20 = f32[8,96,128]{2,1,0:T(8,128)S(1)} all-to-all(f32[8,96,128]{2,1,0:T(8,128)S(1)} %get-tuple-element.20), channel_id=1, replica_groups=mesh['xy'=64,'gz'=8] {'gz'}, dimensions={0} | all-to-all | bytes 786432 | tf_op jit(solution)/shard_map/all_to_all | solution.py:510
  46.0 0.4 block_sums.1
  46.4 23.8 %all_to_all.21 = f32[64,3,2,128]{3,2,1,0:T(2,128)S(1)} all-to-all(f32[64,3,2,128]{3,2,1,0:T(2,128)S(1)} %bitcast.7), channel_id=1, replica_groups=mesh['xy'=64,'gz'=8] {'xy'}, dimensions={0} | all-to-all | bytes 393216 | tf_op jit(solution)/shard_map/all_to_all | solution.py:528
  70.1 0.3 ring.1
  70.4 12.7 %all_to_all.22 = f32[16,3,2,128]{3,2,1,0:T(2,128)S(1)} all-to-all(f32[16,3,2,128]{3,2,1,0:T(2,128)S(1)} %bitcast.8), channel_id=1, replica_groups={{0,8,16,24,128,136,144,152,256,264,272,280,384,392,400,408},{32,40,48,5..., dimensions={0} | all-to-all | bytes 98304 | tf_op jit(solution)/shard_map/all_to_all | solution.py:544
  83.0 0.4 solve.1
  83.4 13.9 %all_to_all.23.solved_ref = f32[8,3,2,16,128]{4,3,2,1,0:T(8,128)S(1)} all-to-all(f32[8,3,2,16,128]{4,3,2,1,0:T(8,128)S(1)} %solve.1), channel_id=1, replica_groups=mesh['xy'=64,'gz'=8] {'gz'}, dimensions={0} | all-to-all | bytes 786432 | tf_op jit(solution)/shard_map/all_to_all | solution.py:561
  97.4 1.2 %back_to_y.1 = f32[3,2,16,1024]{3,2,1,0:T(8,128)} custom-call(f32[8,3,2,16,128]{4,3,2,1,0:T(8,128)S(1)} %all_to_all.23.solved_ref, bf16[2,4,256,256]{3,2,1,0:T(8,128)(2,1)S(1)} %copy-done), custom_call_target="tpu_custom_call" | custom-call | tf_op jit(solution)/shard_map/back_to_y/pallas_call | solution.py:563
  (7 shorter events, 0.0 us)
Async XLA Ops:
  0.6 1.0 %copy-start.2 = (f32[3,2,16,1024]{3,2,1,0:T(8,128)S(1)}, f32[3,2,16,1024]{3,2,1,0:T(8,128)}, u32[]{:S(2)}) copy-start(f32[3,2,16,1024]{3,2,1,0:T(8,128)} %pot_hbm.1) | copy-start | bytes 1179652
  1.6 23.9 %copy-start.1 = (f32[4,2,16,1024]{3,2,1,0:T(8,128)S(1)}, f32[4,2,16,1024]{3,2,1,0:T(8,128)}, u32[]{:S(2)}) copy-start(f32[4,2,16,1024]{3,2,1,0:T(8,128)} %prev_ref.1) | copy-start | bytes 1572868
  1.6 23.9 %copy-start.3 = (f32[24,128]{1,0:T(8,128)S(1)}, f32[24,128]{1,0:T(8,128)}, u32[]{:S(2)}) copy-start(f32[24,128]{1,0:T(8,128)} %constant.5.clone.wave_ref) | copy-start | bytes 36868
  1.6 23.9 %copy-start.4 = (f32[4]{0:T(128)S(1)}, f32[4]{0:T(128)}, u32[]{:S(2)}) copy-start(f32[4]{0:T(128)} %diffusivity_ref.3) | copy-start | bytes 52
  1.6 23.9 %copy-start.5 = (s32[4]{0:T(128)S(1)}, s32[4]{0:T(128)}, u32[]{:S(2)}) copy-start(s32[4]{0:T(128)} %charge_ref.3) | copy-start | bytes 52
  3.4 26.3 %copy-start = (bf16[2,4,256,256]{3,2,1,0:T(8,128)(2,1)S(1)}, bf16[2,4,256,256]{3,2,1,0:T(8,128)(2,1)}, u32[]{:S(2)}) copy-start(bf16[2,4,256,256]{3,2,1,0:T(8,128)(2,1)} %constant.4.clone.table_ref) | copy-start | bytes 3145732
  3.4 26.3 %collective-permute-start = (f32[3,5,16,1024]{3,2,1,0:T(8,128)S(1)}, f32[3,5,16,1024]{3,2,1,0:T(8,128)S(1)}, u32[]{:S(2)}, u32[]{:S(2)}) collective-permute-start(f32[3,5,16,1024]{3,2,1,0:T(8,128)S(1)} %get-tuple-element.13.z_far_ref), channel_id=1, source_target_pairs={{1,2},{3,4},{5,6},{2,1},{4,3},{6,5},{9,10},{11,12},{13,14},{10,9},... | collective-permute-start | bytes 2949128 | tf_op jit(solution)/shard_map/ppermute | solution.py:463
  8.1 21.7 %collective-permute-start.3 = (f32[3,5,16,1024]{3,2,1,0:T(8,128)S(1)}, f32[3,5,16,1024]{3,2,1,0:T(8,128)S(1)}, u32[]{:S(2)}, u32[]{:S(2)}) collective-permute-start(f32[3,5,16,1024]{3,2,1,0:T(8,128)S(1)} %get-tuple-element.14.z_near_ref), channel_id=1, source_target_pairs={{0,1},{2,3},{4,5},{6,7},{1,0},{3,2},{5,4},{7,6},{8,9},{10,11},{12,... | collective-permute-start | bytes 2949128 | tf_op jit(solution)/shard_map/ppermute | solution.py:463
  13.1 15.4 %collective-permute-start.1 = (f32[30,1024]{1,0:T(8,128)S(1)}, f32[30,1024]{1,0:T(8,128)S(1)}, u32[]{:S(2)}, u32[]{:S(2)}) collective-permute-start(f32[30,1024]{1,0:T(8,128)S(1)} %get-tuple-element.16.x_far_sent), channel_id=1, source_target_pairs={{8,16},{24,32},{40,48},{56,64},{72,80},{88,96},{104,112},{120,128}... | collective-permute-start | bytes 368648 | tf_op jit(solution)/shard_map/ppermute | solution.py:463
  23.6 6.1 %collective-permute-start.2 = (f32[30,1024]{1,0:T(8,128)S(1)}, f32[30,1024]{1,0:T(8,128)S(1)}, u32[]{:S(2)}, u32[]{:S(2)}) collective-permute-start(f32[30,1024]{1,0:T(8,128)S(1)} %get-tuple-element.17.x_near_sent), channel_id=1, source_target_pairs={{0,8},{16,24},{32,40},{48,56},{64,72},{80,88},{96,104},{112,120},{... | collective-permute-start | bytes 368648 | tf_op jit(solution)/shard_map/ppermute | solution.py:463

commit v3 on v2

--- a/solution.py
+++ b/solution.py
@@ -455,9 +455,12 @@
         in_specs=[hbm] * 2,
         out_specs=(vmem,) * 4,
         scratch_shapes=[pltpu.SemaphoreType.DMA((n_z, n_section, 2))],
-        compiler_params=params(50),
+        compiler_params=params(12),
         name="pack",
-    )(conc_section, potential)
+    )(
+        pltpu.with_memory_space_constraint(conc_section, pltpu.HBM),
+        pltpu.with_memory_space_constraint(potential, pltpu.HBM),
+    )
 
     def swap(value, axis, pairs):
         return lax.ppermute(value, axis, pairs + [(j, i) for i, j in pairs])

time: 99 us -> 97.9 us (0.989)
  no operation moved by 1% of the time
where the time goes in v3:
time: 97.9 us; the launch traced here: 97.6 us
  blocking collectives  63.9 us (65%)
  starting transfers between devices  22.1 us (23%)
  Pallas kernels  9.65 us (10%)
  waiting for transfers between devices  1.18 us (1%)
    all_to_all x1, blocking collectives, on_device(): lax.all_to_all(sums, 'xy', split_axis=0, concat_axis=0, tiled=True)  23.8 us
    ppermute x4, starting transfers between devices, swap(): return lax.ppermute(value, axis, pairs + [(j, i) for i, j in pairs])  22.1 us
    all_to_all x1, blocking collectives, on_device(): lax.all_to_all(solved, 'gz', split_axis=0, concat_axis=0, tiled=True)  13.9 us
    all_to_all x1, blocking collectives, on_device(): lax.all_to_all(modes, 'gz', split_axis=0, concat_axis=0, tiled=True)  13.6 us
    all_to_all x1, blocking collectives, on_device(): lax.all_to_all(entering, 'xy', split_axis=0, concat_axis=0, tiled=True, a...  12.7 us
    pallas_call x1, Pallas kernels, on_device(): pl.pallas_call(inner_kernel, out_shape=(jax.ShapeDtypeStruct(planes, f32)...  2.99 us
    pallas_call x1, Pallas kernels, on_device(): pl.pallas_call(outer_kernel, out_shape=(jax.ShapeDtypeStruct(conc_section...  2.67 us
  transfers between devices with their start and end apart: 4, of which 1 were waited for; matrix products, arithmetic and copies ran while one was open for 0% of the time, Pallas kernels for 3%

profile of v3, /device:TPU:1, one launch (start us, length us, event | category | flops | bytes accessed | tf_op | source)
XLA Modules:
  0.0 97.6 jit_solution(17640253665587365556)
XLA Ops:
  0.6 0.0 copy-start.2
  0.6 0.0 copy-start.4
  0.7 0.0 copy-start.3
  0.7 0.0 copy-start.1
  0.7 1.7 %pack.1 = (f32[3,5,16,1024]{3,2,1,0:T(8,128)S(1)}, f32[3,5,16,1024]{3,2,1,0:T(8,128)S(1)}, f32[30,1024]{1,0:T(8,128)S(1)}, f32[30,1024]{1,0:T(8,128)S(1)}) custom-call(f32[3,4,2,16,1024]{4,3,2,1,0:T(8,128)} %conc_hbm.1, f32[3,2,16,1024]{3,2,1,0:T(8,128)} %pot_hbm.1), custom_call_target="tpu_custom_call" | custom-call | tf_op jit(solution)/shard_map/pack/pallas_call | solution.py:452
  2.4 0.0 copy-start
  2.4 4.6 %collective-permute-start = (f32[3,5,16,1024]{3,2,1,0:T(8,128)S(1)}, f32[3,5,16,1024]{3,2,1,0:T(8,128)S(1)}, u32[]{:S(2)}, u32[]{:S(2)}) collective-permute-start(f32[3,5,16,1024]{3,2,1,0:T(8,128)S(1)} %get-tuple-element.13.z_far_ref), channel_id=1, source_target_pairs={{1,2},{3,4},{5,6},{2,1},{4,3},{6,5},{9,10},{11,12},{13,14},{10,9},... | collective-permute-start | bytes 2949128 | tf_op jit(solution)/shard_map/ppermute | solution.py:466
  7.0 5.0 %collective-permute-start.3 = (f32[3,5,16,1024]{3,2,1,0:T(8,128)S(1)}, f32[3,5,16,1024]{3,2,1,0:T(8,128)S(1)}, u32[]{:S(2)}, u32[]{:S(2)}) collective-permute-start(f32[3,5,16,1024]{3,2,1,0:T(8,128)S(1)} %get-tuple-element.14.z_near_ref), channel_id=1, source_target_pairs={{0,1},{2,3},{4,5},{6,7},{1,0},{3,2},{5,4},{7,6},{8,9},{10,11},{12,... | collective-permute-start | bytes 2949128 | tf_op jit(solution)/shard_map/ppermute | solution.py:466
  12.0 10.5 %collective-permute-start.1 = (f32[30,1024]{1,0:T(8,128)S(1)}, f32[30,1024]{1,0:T(8,128)S(1)}, u32[]{:S(2)}, u32[]{:S(2)}) collective-permute-start(f32[30,1024]{1,0:T(8,128)S(1)} %get-tuple-element.16.x_far_sent), channel_id=1, source_target_pairs={{8,16},{24,32},{40,48},{56,64},{72,80},{88,96},{104,112},{120,128}... | collective-permute-start | bytes 368648 | tf_op jit(solution)/shard_map/ppermute | solution.py:466
  22.5 1.9 %collective-permute-start.2 = (f32[30,1024]{1,0:T(8,128)S(1)}, f32[30,1024]{1,0:T(8,128)S(1)}, u32[]{:S(2)}, u32[]{:S(2)}) collective-permute-start(f32[30,1024]{1,0:T(8,128)S(1)} %get-tuple-element.17.x_near_sent), channel_id=1, source_target_pairs={{0,8},{16,24},{32,40},{48,56},{64,72},{80,88},{96,104},{112,120},{... | collective-permute-start | bytes 368648 | tf_op jit(solution)/shard_map/ppermute | solution.py:466
  24.5 3.0 %inner_faces.1 = (f32[3,4,2,16,1024]{4,3,2,1,0:T(8,128)S(1)}, f32[3,16,128]{2,1,0:T(8,128)S(1)}, f32[2,128]{1,0:T(2,128)S(1)}) custom-call(f32[4]{0:T(128)S(1)} %copy-done.3, s32[4]{0:T(128)S(1)} %copy-done.4, f32[4,2,16,1024]{3,2,1,0:T(8,128)S(1)} %copy-done.1, f32[3,5,16,1024]{3,2,1,0:T(8,128)S(1)} %get-tuple-element.13.z_far_ref, ...), custom_call_target="tpu_custom_call" | custom-call | flops 20000000 | bytes 4500000 | tf_op jit(solution)/shard_map/inner_faces/pallas_call | solution.py:474
  27.5 0.0 collective-permute-done.1.x_far_got
  27.5 1.2 %collective-permute-done.2.x_near_got = f32[30,1024]{1,0:T(8,128)S(1)} collective-permute-done((f32[30,1024]{1,0:T(8,128)S(1)}, f32[30,1024]{1,0:T(8,128)S(1)}, u32[]{:S(2)}, u32[]{:S(2)}) %collective-permute-start.2) | collective-permute-done | bytes 122912 | tf_op jit(solution)/shard_map/ppermute | solution.py:466
  28.7 0.0 collective-permute-done.z_far_got
  28.7 0.0 collective-permute-done.3.z_near_got
  28.7 2.7 %outer_faces.1 = (f32[3,4,2,16,1024]{4,3,2,1,0:T(8,128)}, f32[8,96,128]{2,1,0:T(8,128)S(1)}) custom-call(f32[4]{0:T(128)S(1)} %copy-done.3, s32[4]{0:T(128)S(1)} %copy-done.4, f32[3,4,2,16,1024]{4,3,2,1,0:T(8,128)S(1)} %get-tuple-element.15.part_ref, f32[3,5,16,1024]{3,2,1,0:T(8,128)S(1)} %get-tuple-element.13.z_far_ref, ...), custom_call_target="tpu_custom_call" | custom-call | tf_op jit(solution)/shard_map/outer_faces/pallas_call | solution.py:492
  31.4 13.6 %all_to_all.20 = f32[8,96,128]{2,1,0:T(8,128)S(1)} all-to-all(f32[8,96,128]{2,1,0:T(8,128)S(1)} %get-tuple-element.20), channel_id=1, replica_groups=mesh['xy'=64,'gz'=8] {'gz'}, dimensions={0} | all-to-all | bytes 786432 | tf_op jit(solution)/shard_map/all_to_all | solution.py:513
  44.9 0.4 block_sums.1
  45.3 23.8 %all_to_all.21 = f32[64,3,2,128]{3,2,1,0:T(2,128)S(1)} all-to-all(f32[64,3,2,128]{3,2,1,0:T(2,128)S(1)} %bitcast.7), channel_id=1, replica_groups=mesh['xy'=64,'gz'=8] {'xy'}, dimensions={0} | all-to-all | bytes 393216 | tf_op jit(solution)/shard_map/all_to_all | solution.py:531
  69.1 0.3 ring.1
  69.4 12.7 %all_to_all.22 = f32[16,3,2,128]{3,2,1,0:T(2,128)S(1)} all-to-all(f32[16,3,2,128]{3,2,1,0:T(2,128)S(1)} %bitcast.8), channel_id=1, replica_groups={{0,8,16,24,128,136,144,152,256,264,272,280,384,392,400,408},{32,40,48,5..., dimensions={0} | all-to-all | bytes 98304 | tf_op jit(solution)/shard_map/all_to_all | solution.py:547
  82.0 0.4 solve.1
  82.4 13.9 %all_to_all.23.solved_ref = f32[8,3,2,16,128]{4,3,2,1,0:T(8,128)S(1)} all-to-all(f32[8,3,2,16,128]{4,3,2,1,0:T(8,128)S(1)} %solve.1), channel_id=1, replica_groups=mesh['xy'=64,'gz'=8] {'gz'}, dimensions={0} | all-to-all | bytes 786432 | tf_op jit(solution)/shard_map/all_to_all | solution.py:564
  96.3 1.2 %back_to_y.1 = f32[3,2,16,1024]{3,2,1,0:T(8,128)} custom-call(f32[8,3,2,16,128]{4,3,2,1,0:T(8,128)S(1)} %all_to_all.23.solved_ref, bf16[2,4,256,256]{3,2,1,0:T(8,128)(2,1)S(1)} %copy-done), custom_call_target="tpu_custom_call" | custom-call | tf_op jit(solution)/shard_map/back_to_y/pallas_call | solution.py:566
  (5 shorter events, 0.0 us)
Async XLA Ops:
  0.6 23.8 %copy-start.2 = (f32[24,128]{1,0:T(8,128)S(1)}, f32[24,128]{1,0:T(8,128)}, u32[]{:S(2)}) copy-start(f32[24,128]{1,0:T(8,128)} %constant.5.clone.wave_ref) | copy-start | bytes 36868
  0.6 23.8 %copy-start.4 = (s32[4]{0:T(128)S(1)}, s32[4]{0:T(128)}, u32[]{:S(2)}) copy-start(s32[4]{0:T(128)} %charge_ref.3) | copy-start | bytes 52
  0.7 23.8 %copy-start.3 = (f32[4]{0:T(128)S(1)}, f32[4]{0:T(128)}, u32[]{:S(2)}) copy-start(f32[4]{0:T(128)} %diffusivity_ref.3) | copy-start | bytes 52
  0.7 23.8 %copy-start.1 = (f32[4,2,16,1024]{3,2,1,0:T(8,128)S(1)}, f32[4,2,16,1024]{3,2,1,0:T(8,128)}, u32[]{:S(2)}) copy-start(f32[4,2,16,1024]{3,2,1,0:T(8,128)} %prev_ref.1) | copy-start | bytes 1572868
  2.4 26.3 %copy-start = (bf16[2,4,256,256]{3,2,1,0:T(8,128)(2,1)S(1)}, bf16[2,4,256,256]{3,2,1,0:T(8,128)(2,1)}, u32[]{:S(2)}) copy-start(bf16[2,4,256,256]{3,2,1,0:T(8,128)(2,1)} %constant.4.clone.table_ref) | copy-start | bytes 3145732
  2.4 26.3 %collective-permute-start = (f32[3,5,16,1024]{3,2,1,0:T(8,128)S(1)}, f32[3,5,16,1024]{3,2,1,0:T(8,128)S(1)}, u32[]{:S(2)}, u32[]{:S(2)}) collective-permute-start(f32[3,5,16,1024]{3,2,1,0:T(8,128)S(1)} %get-tuple-element.13.z_far_ref), channel_id=1, source_target_pairs={{1,2},{3,4},{5,6},{2,1},{4,3},{6,5},{9,10},{11,12},{13,14},{10,9},... | collective-permute-start | bytes 2949128 | tf_op jit(solution)/shard_map/ppermute | solution.py:466
  7.0 21.7 %collective-permute-start.3 = (f32[3,5,16,1024]{3,2,1,0:T(8,128)S(1)}, f32[3,5,16,1024]{3,2,1,0:T(8,128)S(1)}, u32[]{:S(2)}, u32[]{:S(2)}) collective-permute-start(f32[3,5,16,1024]{3,2,1,0:T(8,128)S(1)} %get-tuple-element.14.z_near_ref), channel_id=1, source_target_pairs={{0,1},{2,3},{4,5},{6,7},{1,0},{3,2},{5,4},{7,6},{8,9},{10,11},{12,... | collective-permute-start | bytes 2949128 | tf_op jit(solution)/shard_map/ppermute | solution.py:466
  12.0 15.5 %collective-permute-start.1 = (f32[30,1024]{1,0:T(8,128)S(1)}, f32[30,1024]{1,0:T(8,128)S(1)}, u32[]{:S(2)}, u32[]{:S(2)}) collective-permute-start(f32[30,1024]{1,0:T(8,128)S(1)} %get-tuple-element.16.x_far_sent), channel_id=1, source_target_pairs={{8,16},{24,32},{40,48},{56,64},{72,80},{88,96},{104,112},{120,128}... | collective-permute-start | bytes 368648 | tf_op jit(solution)/shard_map/ppermute | solution.py:466
  22.5 6.1 %collective-permute-start.2 = (f32[30,1024]{1,0:T(8,128)S(1)}, f32[30,1024]{1,0:T(8,128)S(1)}, u32[]{:S(2)}, u32[]{:S(2)}) collective-permute-start(f32[30,1024]{1,0:T(8,128)S(1)} %get-tuple-element.17.x_near_sent), channel_id=1, source_target_pairs={{0,8},{16,24},{32,40},{48,56},{64,72},{80,88},{96,104},{112,120},{... | collective-permute-start | bytes 368648 | tf_op jit(solution)/shard_map/ppermute | solution.py:466

commit v4 on v3

--- a/solution.py
+++ b/solution.py
@@ -63,14 +63,13 @@
     return (far - near) + gain * (near + far)
 
 
-def split_dot(rows, table_ref, pair, contract):
+def split_dot(rows, table_ref, pair):
     count = rows.shape[0]
     high = rows.astype(jnp.bfloat16)
     low = (rows - high.astype(jnp.float32)).astype(jnp.bfloat16)
 
     def product(a, b):
-        dims = (((1,), (contract,)), ((), ()))
-        return lax.dot_general(a, b, dims, preferred_element_type=jnp.float32)
+        return jnp.dot(a, b, preferred_element_type=jnp.float32)
 
     main = product(jnp.concatenate([low, high], axis=0), table_ref[0, pair])
     return (product(high, table_ref[1, pair]) + main[:count]) + main[count:]
@@ -95,7 +94,7 @@
     ]
     blocks = [None] * 8
     for pair, columns in enumerate(inputs):
-        out = split_dot(jnp.concatenate(columns, axis=1), table_ref, pair, 0)
+        out = split_dot(jnp.concatenate(columns, axis=1), table_ref, pair)
         blocks[pair], blocks[8 - pair if pair else 4] = halves(out)
     return blocks
 
@@ -104,7 +103,7 @@
     outs = []
     for pair in range(4):
         columns = jnp.concatenate([blocks[pair], blocks[8 - pair if pair else 4]], axis=1)
-        outs.append(halves(split_dot(columns, table_ref, pair, 1)))
+        outs.append(halves(split_dot(columns, table_ref, pair)))
     (p0, p4), (c1, q1), (c2, q2), (c3, q3) = outs
     even, odd = p0 + p4, p0 - p4
     m = diagonal * (c1 - c3)
@@ -146,23 +145,24 @@
     n_section, n_species, depth, rows, _ = conc_hbm.shape
     z_far = far_layer(depth)
     x_far = far_row(rows)
+    layers = ((z_far, z_far_ref), (depth - 1 - z_far, z_near_ref))
     copies = []
-    for q, (z, ref) in enumerate(((z_far, z_far_ref), (depth - 1 - z_far, z_near_ref))):
-        for j in range(n_section):
-            pair = [
+    for j in range(n_section):
+        copies.append([])
+        for q, (z, ref) in enumerate(layers):
+            copies[j] += [
                 pltpu.make_async_copy(
                     conc_hbm.at[j, :, z], ref.at[j, 0:n_species], sems.at[q, j, 0]
                 ),
                 pltpu.make_async_copy(pot_hbm.at[j, z], ref.at[j, n_species], sems.at[q, j, 1]),
             ]
-            for copy in pair:
-                copy.start()
-            copies.extend(pair)
-    for copy in copies:
-        copy.wait()
-    for x, out_ref in ((x_far, x_far_ref), (rows - 1 - x_far, x_near_ref)):
-        for j in range(n_section):
-            for q, ref in enumerate((z_far_ref, z_near_ref)):
+        for copy in copies[j]:
+            copy.start()
+    for j in range(n_section):
+        for copy in copies[j]:
+            copy.wait()
+        for x, out_ref in ((x_far, x_far_ref), (rows - 1 - x_far, x_near_ref)):
+            for q, (_, ref) in enumerate(layers):
                 for s in range(n_species + 1):
                     to = edge_row(n_section, n_species, depth, j, s, q)
                     out_ref[to : to + 1, :] = ref[j, s, pl.ds(x, 1), :]
@@ -176,7 +176,7 @@
 
 def inner_kernel(
     diffusivity_ref, charge_ref, prev_ref, z_far_ref, z_near_ref, wave_ref,
-    out_ref, decay_ref, own_ref, step_ref, between_ref,
+    out_ref, rhs_ref, decay_ref, own_ref, step_ref, between_ref,
 ):
     n_section, n_species, depth, rows, y_cells = out_ref.shape
     row = lax.broadcasted_iota(jnp.int32, (rows, y_cells), 0)
@@ -187,6 +187,7 @@
             p = ref[j, n_species]
             step_ref[j, q, 0] = p - pltpu.roll(p, 1, 0)
             step_ref[j, q, 1] = pltpu.roll(p, y_cells - 1, 1) - p
+            rhs_ref[j, q] = screening * p
         between_ref[j] = z_near_ref[j, n_species] - z_far_ref[j, n_species]
 
     def species(s, carry):
@@ -212,7 +213,9 @@
                 update = inverse[i] * (prev - c)
                 for j in range(n_section):
                     update = update + coef[i][j] * totals[j][q]
-                out_ref[i, s, q] = c + update
+                update = c + update
+                out_ref[i, s, q] = update
+                rhs_ref[i, q] += (2.0 * half) * update
         return carry
 
     lax.fori_loop(0, n_species, species, 0)
@@ -231,14 +234,18 @@
 
 
 def outer_kernel(
-    diffusivity_ref, charge_ref, part_ref, z_far_ref, z_near_ref, z_far_got,
+    diffusivity_ref, charge_ref, part_ref, rhs_part_ref, z_far_ref, z_near_ref, z_far_got,
     x_far_sent, x_far_got, x_near_sent, x_near_got, z_near_got, table_ref,
-    out_hbm, modes_ref, out_ref, rhs_ref, edge_ref, sems,
+    out_hbm, modes_ref, out_ref, rhs_ref, edge_ref, step_ref, sems,
 ):
     n_section, n_species, depth, rows, y_cells = part_ref.shape
     planes = n_species * depth
+    pairs = ((z_far_ref, z_far_got), (z_near_ref, z_near_got))
+    charge = [charge_ref[s].astype(jnp.float32) for s in range(n_species)]
     kind = lax.broadcasted_iota(jnp.int32, (planes, y_cells), 0) // depth
     by_row = [coefficients(diffusivity_ref, s)[1] for s in range(n_species)]
+    z_far = far_layer(depth)
+    x_far = far_row(rows)
 
     def by_species(values):
         total = jnp.full((planes, y_cells), values[0], jnp.float32)
@@ -246,7 +253,11 @@
             total = jnp.where(kind == s, values[s], total)
         return total
 
-    half_rows = by_species([0.5 * charge_ref[s].astype(jnp.float32) for s in range(n_species)])
+    for i in range(n_section):
+        for q, (own, got) in enumerate(pairs):
+            step_ref[i, q] = got[i, n_species] - own[i, n_species]
+            rhs_ref[i, q] = rhs_part_ref[i, q]
+    charge_rows = by_species(charge)
     sides = ((x_near_sent, x_near_got), (x_far_sent, x_far_got))
     faces = []
     for near, far in sides:
@@ -255,45 +266,41 @@
             step = far[base : base + depth, :] - near[base : base + depth, :]
             step = jnp.concatenate([step] * n_species, axis=0)
             at = slice(j * planes, (j + 1) * planes)
-            faces.append(face(near[at, :], far[at, :], half_rows * step))
+            faces.append(face(near[at, :], far[at, :], 0.5 * charge_rows * step))
+    edge_rows = (rows - 1 - x_far, x_far)
     for i in range(n_section):
         weights = [by_species([by_row[s][i][j] for s in range(n_species)]) for j in range(n_section)]
-        for side in range(2):
+        for side, x in enumerate(edge_rows):
             update = weights[0] * faces[side * n_section]
             for j in range(1, n_section):
                 update = update + weights[j] * faces[side * n_section + j]
             edge_ref[side, i * planes : (i + 1) * planes, :] = update
-
-    pairs = ((z_far_ref, z_far_got), (z_near_ref, z_near_got))
-    for i in range(n_section):
-        for q in range(depth):
-            rhs_ref[i, q] = screening * pairs[q][0][i, n_species]
-    row = lax.broadcasted_iota(jnp.int32, (rows, y_cells), 0)
-    z_far = far_layer(depth)
-    x_far = far_row(rows)
-    at_x = (row == rows - 1 - x_far, row == x_far)
+            update = charge_rows * update
+            total = update[0:depth]
+            for s in range(1, n_species):
+                total = total + update[s * depth : (s + 1) * depth]
+            for q in range(depth):
+                rhs_ref[i, q, pl.ds(x, 1), :] += total[q : q + 1]
 
     def store(s, q):
         z = z_far if q == 0 else depth - 1 - z_far
         return pltpu.make_async_copy(out_ref.at[:, s, q], out_hbm.at[:, s, z], sems.at[s, q])
 
     def species(s, carry):
-        half = 0.5 * charge_ref[s].astype(jnp.float32)
+        q_s = charge_ref[s].astype(jnp.float32)
+        half = 0.5 * q_s
         _, coef = coefficients(diffusivity_ref, s)
         for q, (own, got) in enumerate(pairs):
-            faces = []
-            for j in range(n_section):
-                step = got[j, n_species] - own[j, n_species]
-                faces.append(face(own[j, s], got[j, s], half * step))
+            faces = [face(own[j, s], got[j, s], half * step_ref[j, q]) for j in range(n_section)]
             for i in range(n_section):
-                at = pl.ds(i * planes + s * depth + q, 1)
-                update = part_ref[i, s, q]
-                for side in range(2):
-                    update = update + jnp.where(at_x[side], edge_ref[side, at, :], 0.0)
-                for j in range(n_section):
+                update = coef[i][0] * faces[0]
+                for j in range(1, n_section):
                     update = update + coef[i][j] * faces[j]
-                out_ref[i, s, q] = update
-                rhs_ref[i, q] += (2.0 * half) * update
+                out_ref[i, s, q] = part_ref[i, s, q] + update
+                rhs_ref[i, q] += q_s * update
+                at = pl.ds((i * n_species + s) * depth + q, 1)
+                for side, x in enumerate(edge_rows):
+                    out_ref[i, s, q, pl.ds(x, 1), :] += edge_ref[side, at, :]
             store(s, q).start()
         return carry
 
@@ -368,32 +375,44 @@
 
 def ring_kernel(n_section, own_ref, sums_ref, out_ref, all_ref):
     per = 2 * n_section
-    n_xy = sums_ref.shape[0] // per
+    n_rings = sums_ref.shape[0] // (per * ring)
     rho = jnp.broadcast_to(own_ref[0:1, :], (n_section, lanes))
+    around = power(rho, ring)
     scale = own_ref[1:2, :]
 
-    def ahead_sum(d):
-        return sums_ref[d * per : d * per + n_section, :]
-
-    def back_sum(d):
-        return sums_ref[d * per + n_section : (d + 1) * per, :]
-
-    ahead = ahead_sum(0)
-    back = back_sum(n_xy - 1)
-    for d in range(1, n_xy):
-        ahead = ahead * rho + ahead_sum(d)
-        back = back * rho + back_sum(n_xy - 1 - d)
-    ahead = ahead * scale
-    back = back * scale
-    for d in range(n_xy):
-        e = n_xy - 1 - d
-        all_ref[d * per : d * per + n_section, :] = ahead
-        all_ref[e * per + n_section : (e + 1) * per, :] = back
-        ahead = ahead * rho + ahead_sum(d)
-        back = back * rho + back_sum(e)
+    def ahead_sum(y, z):
+        at = (y * ring + z) * per
+        return sums_ref[at : at + n_section, :]
+
+    def back_sum(y, z):
+        at = (y * ring + z) * per + n_section
+        return sums_ref[at : at + n_section, :]
+
+    ahead, back = [], []
+    for y in range(n_rings):
+        forth, aback = ahead_sum(y, 0), back_sum(y, ring - 1)
+        for z in range(1, ring):
+            forth = forth * rho + ahead_sum(y, z)
+            aback = aback * rho + back_sum(y, ring - 1 - z)
+        ahead.append(forth)
+        back.append(aback)
+    for y in range(n_rings):
+        forth, aback = ahead[y], back[y]
+        for distance in range(n_rings - 1, 0, -1):
+            forth = forth * around + ahead[(y - distance) % n_rings]
+            aback = aback * around + back[(y + distance) % n_rings]
+        forth, aback = forth * scale, aback * scale
+        for z in range(ring):
+            at = (y * ring + z) * per
+            all_ref[at : at + n_section, :] = forth
+            forth = forth * rho + ahead_sum(y, z)
+            e = ring - 1 - z
+            at = (y * ring + e) * per + n_section
+            all_ref[at : at + n_section, :] = aback
+            aback = aback * rho + back_sum(y, e)
     mine = lax.axis_index("xy") % ring // group
     span = group * per
-    for y in range(n_xy // ring):
+    for y in range(n_rings):
         first = pl.multiple_of(y * ring * per + mine * span, 8)
         out_ref[y * span : (y + 1) * span, :] = all_ref[pl.ds(first, span), :]
 
@@ -419,15 +438,23 @@
             out_ref[g, i, q] = plane
 
 
-def final_kernel(solved_ref, table_ref, out_ref):
+def final_kernel(solved_ref, table_ref, out_hbm, out_ref, sems):
     n_gz, n_section, n_z, rows, _ = solved_ref.shape
     z_far = far_layer(n_z)
     blocks = [solved_ref[g].reshape(n_section * n_z * rows, lanes) for g in range(n_gz)]
-    for a, block in enumerate(from_modes(blocks, table_ref)):
-        block = block.reshape(n_section, n_z, rows, lanes)
-        for i in range(n_section):
-            for q, z in enumerate((z_far, n_z - 1 - z_far)):
-                out_ref[i, z, :, a * lanes : (a + 1) * lanes] = block[i, q]
+    fields = from_modes(blocks, table_ref)
+    copies = []
+    for i in range(n_section):
+        for q, z in enumerate((z_far, n_z - 1 - z_far)):
+            at = (i * n_z + q) * rows
+            for a, field in enumerate(fields):
+                out_ref[i, q, :, a * lanes : (a + 1) * lanes] = field[at : at + rows]
+            copies.append(
+                pltpu.make_async_copy(out_ref.at[i, q], out_hbm.at[i, z], sems.at[i, q])
+            )
+            copies[-1].start()
+    for copy in copies:
+        copy.wait()
 
 
 def on_device(conc_prev, conc_section, potential, diffusivity, charges):
@@ -443,7 +470,8 @@
     def params(mib):
         return pltpu.CompilerParams(vmem_limit_bytes=mib * 1024 * 1024)
 
-    table = jnp.asarray(hartley_tables(y_cells))
+    tables = hartley_tables(y_cells)
+    table, table_back = jnp.asarray(tables), jnp.asarray(tables.swapaxes(2, 3))
     sine = sine_matrix(depth)
     wave = jnp.asarray(wave_table(depth, y_cells))
 
@@ -471,15 +499,17 @@
     z_near_in = swap(z_near_out, "gz", [(i, i + 1) for i in range(0, n_gz, 2)])
 
     planes = (n_section, n_species, n_z, rows, y_cells)
-    part, decay_here, own = pl.pallas_call(
+    rhs_shape = (n_section, n_z, rows, y_cells)
+    part, rhs_part, decay_here, own = pl.pallas_call(
         inner_kernel,
         out_shape=(
             jax.ShapeDtypeStruct(planes, f32),
+            jax.ShapeDtypeStruct(rhs_shape, f32),
             jax.ShapeDtypeStruct((3, depth, lanes), f32),
             jax.ShapeDtypeStruct((2, lanes), f32),
         ),
         in_specs=[smem] * 2 + [vmem] * 4,
-        out_specs=(vmem, vmem, vmem),
+        out_specs=(vmem,) * 4,
         scratch_shapes=[
             pltpu.VMEM((n_section, n_z, 2, rows, y_cells), f32),
             pltpu.VMEM((n_section, rows, y_cells), f32),
@@ -495,18 +525,19 @@
             jax.ShapeDtypeStruct(conc_section.shape, f32),
             jax.ShapeDtypeStruct((n_gz, n_section * n_z * rows, lanes), f32),
         ),
-        in_specs=[smem] * 2 + [vmem] * 10,
+        in_specs=[smem] * 2 + [vmem] * 11,
         out_specs=(hbm, vmem),
         scratch_shapes=[
             pltpu.VMEM(planes, f32),
-            pltpu.VMEM((n_section, n_z, rows, y_cells), f32),
+            pltpu.VMEM(rhs_shape, f32),
             pltpu.VMEM((2, n_section * n_species * n_z, y_cells), f32),
+            pltpu.VMEM(rhs_shape, f32),
             pltpu.SemaphoreType.DMA((n_species, n_z)),
         ],
         compiler_params=params(24),
         name="outer_faces",
     )(
-        diffusivity, charges, part, z_far_out, z_near_out, z_far_in,
+        diffusivity, charges, part, rhs_part, z_far_out, z_near_out, z_far_in,
         x_far_out, x_far_in, x_near_out, x_near_in, z_near_in, table,
     )
 
@@ -567,10 +598,14 @@
         final_kernel,
         out_shape=jax.ShapeDtypeStruct(potential.shape, f32),
         in_specs=[vmem] * 2,
-        out_specs=vmem,
+        out_specs=hbm,
+        scratch_shapes=[
+            pltpu.VMEM(potential.shape, f32),
+            pltpu.SemaphoreType.DMA((n_section, n_z)),
+        ],
         compiler_params=params(12),
         name="back_to_y",
-    )(returned, table)
+    )(returned, table_back)
     return (conc_new, potential_new)
 
 

time: 97.9 us -> 97.5 us (level)
  no operation moved by 1% of the time
where the time goes in v4:
time: 97.5 us; the launch traced here: 97.1 us
  blocking collectives  63.9 us (66%)
  starting transfers between devices  22.1 us (23%)
  Pallas kernels  9.3 us (10%)
  waiting for transfers between devices  1.06 us (1%)
    all_to_all x1, blocking collectives, on_device(): lax.all_to_all(sums, 'xy', split_axis=0, concat_axis=0, tiled=True)  23.8 us
    ppermute x4, starting transfers between devices, swap(): return lax.ppermute(value, axis, pairs + [(j, i) for i, j in pairs])  22.1 us
    all_to_all x1, blocking collectives, on_device(): lax.all_to_all(solved, 'gz', split_axis=0, concat_axis=0, tiled=True)  13.9 us
    all_to_all x1, blocking collectives, on_device(): lax.all_to_all(modes, 'gz', split_axis=0, concat_axis=0, tiled=True)  13.6 us
    all_to_all x1, blocking collectives, on_device(): lax.all_to_all(entering, 'xy', split_axis=0, concat_axis=0, tiled=True, a...  12.7 us
    pallas_call x1, Pallas kernels, on_device(): pl.pallas_call(inner_kernel, out_shape=(jax.ShapeDtypeStruct(planes, f32)...  3.11 us
    pallas_call x1, Pallas kernels, on_device(): pl.pallas_call(outer_kernel, out_shape=(jax.ShapeDtypeStruct(conc_section...  2.52 us
  transfers between devices with their start and end apart: 4, of which 1 were waited for; matrix products, arithmetic and copies ran while one was open for 0% of the time, Pallas kernels for 3%

profile of v4, /device:TPU:1, one launch (start us, length us, event | category | flops | bytes accessed | tf_op | source)
XLA Modules:
  0.0 97.1 jit_solution(13912986383625109924)
XLA Ops:
  0.6 0.0 copy-start.3
  0.6 0.0 copy-start.5
  0.7 0.0 copy-start.4
  0.7 0.0 copy-start.2
  0.7 1.7 %pack.1 = (f32[3,5,16,1024]{3,2,1,0:T(8,128)S(1)}, f32[3,5,16,1024]{3,2,1,0:T(8,128)S(1)}, f32[30,1024]{1,0:T(8,128)S(1)}, f32[30,1024]{1,0:T(8,128)S(1)}) custom-call(f32[3,4,2,16,1024]{4,3,2,1,0:T(8,128)} %conc_hbm.1, f32[3,2,16,1024]{3,2,1,0:T(8,128)} %pot_hbm.1), custom_call_target="tpu_custom_call" | custom-call | tf_op jit(solution)/shard_map/pack/pallas_call | solution.py:480
  2.3 0.0 copy-start.1
  2.3 4.6 %collective-permute-start = (f32[3,5,16,1024]{3,2,1,0:T(8,128)S(1)}, f32[3,5,16,1024]{3,2,1,0:T(8,128)S(1)}, u32[]{:S(2)}, u32[]{:S(2)}) collective-permute-start(f32[3,5,16,1024]{3,2,1,0:T(8,128)S(1)} %get-tuple-element.14.z_far_ref), channel_id=1, source_target_pairs={{1,2},{3,4},{5,6},{2,1},{4,3},{6,5},{9,10},{11,12},{13,14},{10,9},... | collective-permute-start | bytes 2949128 | tf_op jit(solution)/shard_map/ppermute | solution.py:494
  7.0 5.0 %collective-permute-start.3 = (f32[3,5,16,1024]{3,2,1,0:T(8,128)S(1)}, f32[3,5,16,1024]{3,2,1,0:T(8,128)S(1)}, u32[]{:S(2)}, u32[]{:S(2)}) collective-permute-start(f32[3,5,16,1024]{3,2,1,0:T(8,128)S(1)} %get-tuple-element.15.z_near_ref), channel_id=1, source_target_pairs={{0,1},{2,3},{4,5},{6,7},{1,0},{3,2},{5,4},{7,6},{8,9},{10,11},{12,... | collective-permute-start | bytes 2949128 | tf_op jit(solution)/shard_map/ppermute | solution.py:494
  12.0 10.5 %collective-permute-start.1 = (f32[30,1024]{1,0:T(8,128)S(1)}, f32[30,1024]{1,0:T(8,128)S(1)}, u32[]{:S(2)}, u32[]{:S(2)}) collective-permute-start(f32[30,1024]{1,0:T(8,128)S(1)} %get-tuple-element.18.x_far_sent), channel_id=1, source_target_pairs={{8,16},{24,32},{40,48},{56,64},{72,80},{88,96},{104,112},{120,128}... | collective-permute-start | bytes 368648 | tf_op jit(solution)/shard_map/ppermute | solution.py:494
  22.5 1.9 %collective-permute-start.2 = (f32[30,1024]{1,0:T(8,128)S(1)}, f32[30,1024]{1,0:T(8,128)S(1)}, u32[]{:S(2)}, u32[]{:S(2)}) collective-permute-start(f32[30,1024]{1,0:T(8,128)S(1)} %get-tuple-element.19.x_near_sent), channel_id=1, source_target_pairs={{0,8},{16,24},{32,40},{48,56},{64,72},{80,88},{96,104},{112,120},{... | collective-permute-start | bytes 368648 | tf_op jit(solution)/shard_map/ppermute | solution.py:494
  24.5 3.1 %inner_faces.1 = (f32[3,4,2,16,1024]{4,3,2,1,0:T(8,128)S(1)}, f32[3,2,16,1024]{3,2,1,0:T(8,128)S(1)}, f32[3,16,128]{2,1,0:T(8,128)S(1)}, f32[2,128]{1,0:T(2,128)S(1)}) custom-call(f32[4]{0:T(128)S(1)} %copy-done.4, s32[4]{0:T(128)S(1)} %copy-done.5, f32[4,2,16,1024]{3,2,1,0:T(8,128)S(1)} %copy-done.2, f32[3,5,16,1024]{3,2,1,0:T(8,128)S(1)} %get-tuple-element.14.z_far_ref, ...), custom_call_target="tpu_custom_call" | custom-call | flops 20000000 | bytes 4500000 | tf_op jit(solution)/shard_map/inner_faces/pallas_call | solution.py:503
  27.6 0.0 collective-permute-done.1.x_far_got
  27.6 1.1 %collective-permute-done.2.x_near_got = f32[30,1024]{1,0:T(8,128)S(1)} collective-permute-done((f32[30,1024]{1,0:T(8,128)S(1)}, f32[30,1024]{1,0:T(8,128)S(1)}, u32[]{:S(2)}, u32[]{:S(2)}) %collective-permute-start.2) | collective-permute-done | bytes 122912 | tf_op jit(solution)/shard_map/ppermute | solution.py:494
  28.6 0.0 collective-permute-done.z_far_got
  28.6 0.0 collective-permute-done.3.z_near_got
  28.7 2.5 %outer_faces.1 = (f32[3,4,2,16,1024]{4,3,2,1,0:T(8,128)}, f32[8,96,128]{2,1,0:T(8,128)S(1)}) custom-call(f32[4]{0:T(128)S(1)} %copy-done.4, s32[4]{0:T(128)S(1)} %copy-done.5, f32[3,4,2,16,1024]{4,3,2,1,0:T(8,128)S(1)} %get-tuple-element.16.part_ref, f32[3,2,16,1024]{3,2,1,0:T(8,128)S(1)} %get-tuple-element.17.rhs_part_ref, ...), custom_call_target="tpu_custom_call" | custom-call | tf_op jit(solution)/shard_map/outer_faces/pallas_call | solution.py:522
  31.2 13.6 %all_to_all.20 = f32[8,96,128]{2,1,0:T(8,128)S(1)} all-to-all(f32[8,96,128]{2,1,0:T(8,128)S(1)} %get-tuple-element.22), channel_id=1, replica_groups=mesh['xy'=64,'gz'=8] {'gz'}, dimensions={0} | all-to-all | bytes 786432 | tf_op jit(solution)/shard_map/all_to_all | solution.py:544
  44.7 0.4 block_sums.1
  45.1 23.8 %all_to_all.21 = f32[64,3,2,128]{3,2,1,0:T(2,128)S(1)} all-to-all(f32[64,3,2,128]{3,2,1,0:T(2,128)S(1)} %bitcast.7), channel_id=1, replica_groups=mesh['xy'=64,'gz'=8] {'xy'}, dimensions={0} | all-to-all | bytes 393216 | tf_op jit(solution)/shard_map/all_to_all | solution.py:562
  68.9 0.1 ring.1
  69.0 12.7 %all_to_all.22 = f32[16,3,2,128]{3,2,1,0:T(2,128)S(1)} all-to-all(f32[16,3,2,128]{3,2,1,0:T(2,128)S(1)} %bitcast.8), channel_id=1, replica_groups={{0,8,16,24,128,136,144,152,256,264,272,280,384,392,400,408},{32,40,48,5..., dimensions={0} | all-to-all | bytes 98304 | tf_op jit(solution)/shard_map/all_to_all | solution.py:578
  81.7 0.4 solve.1
  82.1 13.9 %all_to_all.23.solved_ref = f32[8,3,2,16,128]{4,3,2,1,0:T(8,128)S(1)} all-to-all(f32[8,3,2,16,128]{4,3,2,1,0:T(8,128)S(1)} %solve.1), channel_id=1, replica_groups=mesh['xy'=64,'gz'=8] {'gz'}, dimensions={0} | all-to-all | bytes 786432 | tf_op jit(solution)/shard_map/all_to_all | solution.py:595
  96.0 1.1 %back_to_y.1 = f32[3,2,16,1024]{3,2,1,0:T(8,128)} custom-call(f32[8,3,2,16,128]{4,3,2,1,0:T(8,128)S(1)} %all_to_all.23.solved_ref, bf16[2,4,256,256]{3,2,1,0:T(8,128)(2,1)S(1)} %copy-done), custom_call_target="tpu_custom_call" | custom-call | tf_op jit(solution)/shard_map/back_to_y/pallas_call | solution.py:597
  (7 shorter events, 0.0 us)
Async XLA Ops:
  0.6 23.8 %copy-start.3 = (f32[24,128]{1,0:T(8,128)S(1)}, f32[24,128]{1,0:T(8,128)}, u32[]{:S(2)}) copy-start(f32[24,128]{1,0:T(8,128)} %constant.8.clone.wave_ref) | copy-start | bytes 36868
  0.6 23.8 %copy-start.5 = (s32[4]{0:T(128)S(1)}, s32[4]{0:T(128)}, u32[]{:S(2)}) copy-start(s32[4]{0:T(128)} %charge_ref.3) | copy-start | bytes 52
  0.7 23.8 %copy-start.4 = (f32[4]{0:T(128)S(1)}, f32[4]{0:T(128)}, u32[]{:S(2)}) copy-start(f32[4]{0:T(128)} %diffusivity_ref.3) | copy-start | bytes 52
  0.7 23.8 %copy-start.2 = (f32[4,2,16,1024]{3,2,1,0:T(8,128)S(1)}, f32[4,2,16,1024]{3,2,1,0:T(8,128)}, u32[]{:S(2)}) copy-start(f32[4,2,16,1024]{3,2,1,0:T(8,128)} %prev_ref.1) | copy-start | bytes 1572868
  2.3 26.3 %copy-start.1 = (bf16[2,4,256,256]{3,2,1,0:T(8,128)(2,1)S(1)}, bf16[2,4,256,256]{3,2,1,0:T(8,128)(2,1)}, u32[]{:S(2)}) copy-start(bf16[2,4,256,256]{3,2,1,0:T(8,128)(2,1)} %constant.6.clone.table_ref) | copy-start | bytes 3145732
  2.3 26.3 %collective-permute-start = (f32[3,5,16,1024]{3,2,1,0:T(8,128)S(1)}, f32[3,5,16,1024]{3,2,1,0:T(8,128)S(1)}, u32[]{:S(2)}, u32[]{:S(2)}) collective-permute-start(f32[3,5,16,1024]{3,2,1,0:T(8,128)S(1)} %get-tuple-element.14.z_far_ref), channel_id=1, source_target_pairs={{1,2},{3,4},{5,6},{2,1},{4,3},{6,5},{9,10},{11,12},{13,14},{10,9},... | collective-permute-start | bytes 2949128 | tf_op jit(solution)/shard_map/ppermute | solution.py:494
  7.0 21.7 %collective-permute-start.3 = (f32[3,5,16,1024]{3,2,1,0:T(8,128)S(1)}, f32[3,5,16,1024]{3,2,1,0:T(8,128)S(1)}, u32[]{:S(2)}, u32[]{:S(2)}) collective-permute-start(f32[3,5,16,1024]{3,2,1,0:T(8,128)S(1)} %get-tuple-element.15.z_near_ref), channel_id=1, source_target_pairs={{0,1},{2,3},{4,5},{6,7},{1,0},{3,2},{5,4},{7,6},{8,9},{10,11},{12,... | collective-permute-start | bytes 2949128 | tf_op jit(solution)/shard_map/ppermute | solution.py:494
  12.0 15.6 %collective-permute-start.1 = (f32[30,1024]{1,0:T(8,128)S(1)}, f32[30,1024]{1,0:T(8,128)S(1)}, u32[]{:S(2)}, u32[]{:S(2)}) collective-permute-start(f32[30,1024]{1,0:T(8,128)S(1)} %get-tuple-element.18.x_far_sent), channel_id=1, source_target_pairs={{8,16},{24,32},{40,48},{56,64},{72,80},{88,96},{104,112},{120,128}... | collective-permute-start | bytes 368648 | tf_op jit(solution)/shard_map/ppermute | solution.py:494
  22.5 6.1 %collective-permute-start.2 = (f32[30,1024]{1,0:T(8,128)S(1)}, f32[30,1024]{1,0:T(8,128)S(1)}, u32[]{:S(2)}, u32[]{:S(2)}) collective-permute-start(f32[30,1024]{1,0:T(8,128)S(1)} %get-tuple-element.19.x_near_sent), channel_id=1, source_target_pairs={{0,8},{16,24},{32,40},{48,56},{64,72},{80,88},{96,104},{112,120},{... | collective-permute-start | bytes 368648 | tf_op jit(solution)/shard_map/ppermute | solution.py:494
  44.7 51.2 %copy-start = (bf16[2,4,256,256]{3,2,1,0:T(8,128)(2,1)S(1)}, bf16[2,4,256,256]{3,2,1,0:T(8,128)(2,1)}, u32[]{:S(2)}) copy-start(bf16[2,4,256,256]{3,2,1,0:T(8,128)(2,1)} %constant.7.clone.table_ref) | copy-start | bytes 3145732

commit v5 on v4

--- a/solution.py
+++ b/solution.py
@@ -236,7 +236,7 @@
 def outer_kernel(
     diffusivity_ref, charge_ref, part_ref, rhs_part_ref, z_far_ref, z_near_ref, z_far_got,
     x_far_sent, x_far_got, x_near_sent, x_near_got, z_near_got, table_ref,
-    out_hbm, modes_ref, out_ref, rhs_ref, edge_ref, step_ref, sems,
+    out_ref, modes_ref, rhs_ref, edge_ref, step_ref,
 ):
     n_section, n_species, depth, rows, y_cells = part_ref.shape
     planes = n_species * depth
@@ -282,10 +282,6 @@
             for q in range(depth):
                 rhs_ref[i, q, pl.ds(x, 1), :] += total[q : q + 1]
 
-    def store(s, q):
-        z = z_far if q == 0 else depth - 1 - z_far
-        return pltpu.make_async_copy(out_ref.at[:, s, q], out_hbm.at[:, s, z], sems.at[s, q])
-
     def species(s, carry):
         q_s = charge_ref[s].astype(jnp.float32)
         half = 0.5 * q_s
@@ -296,21 +292,18 @@
                 update = coef[i][0] * faces[0]
                 for j in range(1, n_section):
                     update = update + coef[i][j] * faces[j]
-                out_ref[i, s, q] = part_ref[i, s, q] + update
+                z = z_far if q == 0 else depth - 1 - z_far
+                out_ref[i, s, z] = part_ref[i, s, q] + update
                 rhs_ref[i, q] += q_s * update
                 at = pl.ds((i * n_species + s) * depth + q, 1)
                 for side, x in enumerate(edge_rows):
-                    out_ref[i, s, q, pl.ds(x, 1), :] += edge_ref[side, at, :]
-            store(s, q).start()
+                    out_ref[i, s, z, pl.ds(x, 1), :] += edge_ref[side, at, :]
         return carry
 
     lax.fori_loop(0, n_species, species, 0)
     rhs = rhs_ref[...].reshape(n_section * depth * rows, y_cells)
     for g, block in enumerate(to_modes(rhs, table_ref)):
         modes_ref[g] = block
-    for s in range(n_species):
-        for q in range(depth):
-            store(s, q).wait()
 
 
 def layer_of(z, n_z):
@@ -438,7 +431,9 @@
             out_ref[g, i, q] = plane
 
 
-def final_kernel(solved_ref, table_ref, out_hbm, out_ref, sems):
+def final_kernel(solved_ref, table_ref, conc_ref, out_hbm, conc_hbm, out_ref, sems, conc_sem):
+    conc_copy = pltpu.make_async_copy(conc_ref, conc_hbm, conc_sem)
+    conc_copy.start()
     n_gz, n_section, n_z, rows, _ = solved_ref.shape
     z_far = far_layer(n_z)
     blocks = [solved_ref[g].reshape(n_section * n_z * rows, lanes) for g in range(n_gz)]
@@ -455,6 +450,7 @@
             copies[-1].start()
     for copy in copies:
         copy.wait()
+    conc_copy.wait()
 
 
 def on_device(conc_prev, conc_section, potential, diffusivity, charges):
@@ -522,17 +518,15 @@
     conc_new, modes = pl.pallas_call(
         outer_kernel,
         out_shape=(
-            jax.ShapeDtypeStruct(conc_section.shape, f32),
+            pltpu.VMEM(conc_section.shape, f32),
             jax.ShapeDtypeStruct((n_gz, n_section * n_z * rows, lanes), f32),
         ),
         in_specs=[smem] * 2 + [vmem] * 11,
-        out_specs=(hbm, vmem),
+        out_specs=(vmem, vmem),
         scratch_shapes=[
-            pltpu.VMEM(planes, f32),
             pltpu.VMEM(rhs_shape, f32),
             pltpu.VMEM((2, n_section * n_species * n_z, y_cells), f32),
             pltpu.VMEM(rhs_shape, f32),
-            pltpu.SemaphoreType.DMA((n_species, n_z)),
         ],
         compiler_params=params(24),
         name="outer_faces",
@@ -594,18 +588,22 @@
     )(decay_here, hat, enter)
     returned = lax.all_to_all(solved, "gz", split_axis=0, concat_axis=0, tiled=True)
 
-    potential_new = pl.pallas_call(
+    potential_new, conc_new = pl.pallas_call(
         final_kernel,
-        out_shape=jax.ShapeDtypeStruct(potential.shape, f32),
-        in_specs=[vmem] * 2,
-        out_specs=hbm,
+        out_shape=(
+            jax.ShapeDtypeStruct(potential.shape, f32),
+            jax.ShapeDtypeStruct(conc_section.shape, f32),
+        ),
+        in_specs=[vmem] * 3,
+        out_specs=(hbm, hbm),
         scratch_shapes=[
             pltpu.VMEM(potential.shape, f32),
             pltpu.SemaphoreType.DMA((n_section, n_z)),
+            pltpu.SemaphoreType.DMA(()),
         ],
         compiler_params=params(12),
         name="back_to_y",
-    )(returned, table_back)
+    )(returned, table_back, conc_new)
     return (conc_new, potential_new)
 
 

time: 97.5 us -> 97.3 us (level)
  no operation moved by 1% of the time
where the time goes in v5:
time: 97.3 us; the launch traced here: 96.9 us
  blocking collectives  63.9 us (66%)
  starting transfers between devices  22.1 us (23%)
  Pallas kernels  9.09 us (9%)
  waiting for transfers between devices  1.06 us (1%)
    all_to_all x1, blocking collectives, on_device(): lax.all_to_all(sums, 'xy', split_axis=0, concat_axis=0, tiled=True)  23.8 us
    ppermute x4, starting transfers between devices, swap(): return lax.ppermute(value, axis, pairs + [(j, i) for i, j in pairs])  22.1 us
    all_to_all x1, blocking collectives, on_device(): lax.all_to_all(solved, 'gz', split_axis=0, concat_axis=0, tiled=True)  13.9 us
    all_to_all x1, blocking collectives, on_device(): lax.all_to_all(modes, 'gz', split_axis=0, concat_axis=0, tiled=True)  13.6 us
    all_to_all x1, blocking collectives, on_device(): lax.all_to_all(entering, 'xy', split_axis=0, concat_axis=0, tiled=True, a...  12.7 us
    pallas_call x1, Pallas kernels, on_device(): pl.pallas_call(inner_kernel, out_shape=(jax.ShapeDtypeStruct(planes, f32)...  3.11 us
    pallas_call x1, Pallas kernels, on_device(): pl.pallas_call(outer_kernel, out_shape=(pltpu.VMEM(conc_section.shape, f3...  2.11 us
  transfers between devices with their start and end apart: 4, of which 1 were waited for; matrix products, arithmetic and copies ran while one was open for 0% of the time, Pallas kernels for 3%

profile of v5, /device:TPU:1, one launch (start us, length us, event | category | flops | bytes accessed | tf_op | source)
XLA Modules:
  0.0 96.9 jit_solution(6862407381399655175)
XLA Ops:
  0.6 0.0 copy-start.3
  0.6 0.0 copy-start.5
  0.7 0.0 copy-start.4
  0.7 0.0 copy-start.2
  0.7 1.7 %pack.1 = (f32[3,5,16,1024]{3,2,1,0:T(8,128)S(1)}, f32[3,5,16,1024]{3,2,1,0:T(8,128)S(1)}, f32[30,1024]{1,0:T(8,128)S(1)}, f32[30,1024]{1,0:T(8,128)S(1)}) custom-call(f32[3,4,2,16,1024]{4,3,2,1,0:T(8,128)} %conc_hbm.1, f32[3,2,16,1024]{3,2,1,0:T(8,128)} %pot_hbm.1), custom_call_target="tpu_custom_call" | custom-call | tf_op jit(solution)/shard_map/pack/pallas_call | solution.py:476
  2.3 0.0 copy-start.1
  2.3 4.6 %collective-permute-start = (f32[3,5,16,1024]{3,2,1,0:T(8,128)S(1)}, f32[3,5,16,1024]{3,2,1,0:T(8,128)S(1)}, u32[]{:S(2)}, u32[]{:S(2)}) collective-permute-start(f32[3,5,16,1024]{3,2,1,0:T(8,128)S(1)} %get-tuple-element.16.z_far_ref), channel_id=1, source_target_pairs={{1,2},{3,4},{5,6},{2,1},{4,3},{6,5},{9,10},{11,12},{13,14},{10,9},... | collective-permute-start | bytes 2949128 | tf_op jit(solution)/shard_map/ppermute | solution.py:490
  7.0 5.0 %collective-permute-start.3 = (f32[3,5,16,1024]{3,2,1,0:T(8,128)S(1)}, f32[3,5,16,1024]{3,2,1,0:T(8,128)S(1)}, u32[]{:S(2)}, u32[]{:S(2)}) collective-permute-start(f32[3,5,16,1024]{3,2,1,0:T(8,128)S(1)} %get-tuple-element.17.z_near_ref), channel_id=1, source_target_pairs={{0,1},{2,3},{4,5},{6,7},{1,0},{3,2},{5,4},{7,6},{8,9},{10,11},{12,... | collective-permute-start | bytes 2949128 | tf_op jit(solution)/shard_map/ppermute | solution.py:490
  12.0 10.5 %collective-permute-start.1 = (f32[30,1024]{1,0:T(8,128)S(1)}, f32[30,1024]{1,0:T(8,128)S(1)}, u32[]{:S(2)}, u32[]{:S(2)}) collective-permute-start(f32[30,1024]{1,0:T(8,128)S(1)} %get-tuple-element.21.x_far_sent), channel_id=1, source_target_pairs={{8,16},{24,32},{40,48},{56,64},{72,80},{88,96},{104,112},{120,128}... | collective-permute-start | bytes 368648 | tf_op jit(solution)/shard_map/ppermute | solution.py:490
  22.5 1.9 %collective-permute-start.2 = (f32[30,1024]{1,0:T(8,128)S(1)}, f32[30,1024]{1,0:T(8,128)S(1)}, u32[]{:S(2)}, u32[]{:S(2)}) collective-permute-start(f32[30,1024]{1,0:T(8,128)S(1)} %get-tuple-element.22.x_near_sent), channel_id=1, source_target_pairs={{0,8},{16,24},{32,40},{48,56},{64,72},{80,88},{96,104},{112,120},{... | collective-permute-start | bytes 368648 | tf_op jit(solution)/shard_map/ppermute | solution.py:490
  24.5 3.1 %inner_faces.1 = (f32[3,4,2,16,1024]{4,3,2,1,0:T(8,128)S(1)}, f32[3,2,16,1024]{3,2,1,0:T(8,128)S(1)}, f32[3,16,128]{2,1,0:T(8,128)S(1)}, f32[2,128]{1,0:T(2,128)S(1)}) custom-call(f32[4]{0:T(128)S(1)} %copy-done.4, s32[4]{0:T(128)S(1)} %copy-done.5, f32[4,2,16,1024]{3,2,1,0:T(8,128)S(1)} %copy-done.2, f32[3,5,16,1024]{3,2,1,0:T(8,128)S(1)} %get-tuple-element.16.z_far_ref, ...), custom_call_target="tpu_custom_call" | custom-call | flops 20000000 | bytes 4500000 | tf_op jit(solution)/shard_map/inner_faces/pallas_call | solution.py:499
  27.6 0.0 collective-permute-done.1.x_far_got
  27.6 1.1 %collective-permute-done.2.x_near_got = f32[30,1024]{1,0:T(8,128)S(1)} collective-permute-done((f32[30,1024]{1,0:T(8,128)S(1)}, f32[30,1024]{1,0:T(8,128)S(1)}, u32[]{:S(2)}, u32[]{:S(2)}) %collective-permute-start.2) | collective-permute-done | bytes 122912 | tf_op jit(solution)/shard_map/ppermute | solution.py:490
  28.6 0.0 collective-permute-done.z_far_got
  28.6 0.0 collective-permute-done.3.z_near_got
  28.7 2.1 %outer_faces.1 = (f32[3,4,2,16,1024]{4,3,2,1,0:T(8,128)S(1)}, f32[8,96,128]{2,1,0:T(8,128)S(1)}) custom-call(f32[4]{0:T(128)S(1)} %copy-done.4, s32[4]{0:T(128)S(1)} %copy-done.5, f32[3,4,2,16,1024]{4,3,2,1,0:T(8,128)S(1)} %get-tuple-element.19.part_ref, f32[3,2,16,1024]{3,2,1,0:T(8,128)S(1)} %get-tuple-element.20.rhs_part_ref, ...), custom_call_target="tpu_custom_call" | custom-call | tf_op jit(solution)/shard_map/outer_faces/pallas_call | solution.py:518
  30.8 13.6 %all_to_all.20 = f32[8,96,128]{2,1,0:T(8,128)S(1)} all-to-all(f32[8,96,128]{2,1,0:T(8,128)S(1)} %get-tuple-element.23), channel_id=1, replica_groups=mesh['xy'=64,'gz'=8] {'gz'}, dimensions={0} | all-to-all | bytes 786432 | tf_op jit(solution)/shard_map/all_to_all | solution.py:538
  44.3 0.4 block_sums.1
  44.7 23.8 %all_to_all.21 = f32[64,3,2,128]{3,2,1,0:T(2,128)S(1)} all-to-all(f32[64,3,2,128]{3,2,1,0:T(2,128)S(1)} %bitcast.7), channel_id=1, replica_groups=mesh['xy'=64,'gz'=8] {'xy'}, dimensions={0} | all-to-all | bytes 393216 | tf_op jit(solution)/shard_map/all_to_all | solution.py:556
  68.5 0.1 ring.1
  68.6 12.7 %all_to_all.22 = f32[16,3,2,128]{3,2,1,0:T(2,128)S(1)} all-to-all(f32[16,3,2,128]{3,2,1,0:T(2,128)S(1)} %bitcast.8), channel_id=1, replica_groups={{0,8,16,24,128,136,144,152,256,264,272,280,384,392,400,408},{32,40,48,5..., dimensions={0} | all-to-all | bytes 98304 | tf_op jit(solution)/shard_map/all_to_all | solution.py:572
  81.2 0.4 solve.1
  81.6 13.9 %all_to_all.23.solved_ref = f32[8,3,2,16,128]{4,3,2,1,0:T(8,128)S(1)} all-to-all(f32[8,3,2,16,128]{4,3,2,1,0:T(8,128)S(1)} %solve.1), channel_id=1, replica_groups=mesh['xy'=64,'gz'=8] {'gz'}, dimensions={0} | all-to-all | bytes 786432 | tf_op jit(solution)/shard_map/all_to_all | solution.py:589
  95.6 1.3 %back_to_y.1 = (f32[3,2,16,1024]{3,2,1,0:T(8,128)}, f32[3,4,2,16,1024]{4,3,2,1,0:T(8,128)}) custom-call(f32[8,3,2,16,128]{4,3,2,1,0:T(8,128)S(1)} %all_to_all.23.solved_ref, bf16[2,4,256,256]{3,2,1,0:T(8,128)(2,1)S(1)} %copy-done, f32[3,4,2,16,1024]{4,3,2,1,0:T(8,128)S(1)} %get-tuple-element.27.conc_ref), custom_call_target="tpu_custom_call" | custom-call | tf_op jit(solution)/shard_map/back_to_y/pallas_call | solution.py:591
  (7 shorter events, 0.0 us)
Async XLA Ops:
  0.6 23.8 %copy-start.3 = (f32[24,128]{1,0:T(8,128)S(1)}, f32[24,128]{1,0:T(8,128)}, u32[]{:S(2)}) copy-start(f32[24,128]{1,0:T(8,128)} %constant.8.clone.wave_ref) | copy-start | bytes 36868
  0.6 23.8 %copy-start.5 = (s32[4]{0:T(128)S(1)}, s32[4]{0:T(128)}, u32[]{:S(2)}) copy-start(s32[4]{0:T(128)} %charge_ref.3) | copy-start | bytes 52
  0.7 23.8 %copy-start.4 = (f32[4]{0:T(128)S(1)}, f32[4]{0:T(128)}, u32[]{:S(2)}) copy-start(f32[4]{0:T(128)} %diffusivity_ref.3) | copy-start | bytes 52
  0.7 23.8 %copy-start.2 = (f32[4,2,16,1024]{3,2,1,0:T(8,128)S(1)}, f32[4,2,16,1024]{3,2,1,0:T(8,128)}, u32[]{:S(2)}) copy-start(f32[4,2,16,1024]{3,2,1,0:T(8,128)} %prev_ref.1) | copy-start | bytes 1572868
  2.3 26.3 %copy-start.1 = (bf16[2,4,256,256]{3,2,1,0:T(8,128)(2,1)S(1)}, bf16[2,4,256,256]{3,2,1,0:T(8,128)(2,1)}, u32[]{:S(2)}) copy-start(bf16[2,4,256,256]{3,2,1,0:T(8,128)(2,1)} %constant.6.clone.table_ref) | copy-start | bytes 3145732
  2.3 26.3 %collective-permute-start = (f32[3,5,16,1024]{3,2,1,0:T(8,128)S(1)}, f32[3,5,16,1024]{3,2,1,0:T(8,128)S(1)}, u32[]{:S(2)}, u32[]{:S(2)}) collective-permute-start(f32[3,5,16,1024]{3,2,1,0:T(8,128)S(1)} %get-tuple-element.16.z_far_ref), channel_id=1, source_target_pairs={{1,2},{3,4},{5,6},{2,1},{4,3},{6,5},{9,10},{11,12},{13,14},{10,9},... | collective-permute-start | bytes 2949128 | tf_op jit(solution)/shard_map/ppermute | solution.py:490
  7.0 21.7 %collective-permute-start.3 = (f32[3,5,16,1024]{3,2,1,0:T(8,128)S(1)}, f32[3,5,16,1024]{3,2,1,0:T(8,128)S(1)}, u32[]{:S(2)}, u32[]{:S(2)}) collective-permute-start(f32[3,5,16,1024]{3,2,1,0:T(8,128)S(1)} %get-tuple-element.17.z_near_ref), channel_id=1, source_target_pairs={{0,1},{2,3},{4,5},{6,7},{1,0},{3,2},{5,4},{7,6},{8,9},{10,11},{12,... | collective-permute-start | bytes 2949128 | tf_op jit(solution)/shard_map/ppermute | solution.py:490
  12.0 15.6 %collective-permute-start.1 = (f32[30,1024]{1,0:T(8,128)S(1)}, f32[30,1024]{1,0:T(8,128)S(1)}, u32[]{:S(2)}, u32[]{:S(2)}) collective-permute-start(f32[30,1024]{1,0:T(8,128)S(1)} %get-tuple-element.21.x_far_sent), channel_id=1, source_target_pairs={{8,16},{24,32},{40,48},{56,64},{72,80},{88,96},{104,112},{120,128}... | collective-permute-start | bytes 368648 | tf_op jit(solution)/shard_map/ppermute | solution.py:490
  22.5 6.1 %collective-permute-start.2 = (f32[30,1024]{1,0:T(8,128)S(1)}, f32[30,1024]{1,0:T(8,128)S(1)}, u32[]{:S(2)}, u32[]{:S(2)}) collective-permute-start(f32[30,1024]{1,0:T(8,128)S(1)} %get-tuple-element.22.x_near_sent), channel_id=1, source_target_pairs={{0,8},{16,24},{32,40},{48,56},{64,72},{80,88},{96,104},{112,120},{... | collective-permute-start | bytes 368648 | tf_op jit(solution)/shard_map/ppermute | solution.py:490
  44.3 51.2 %copy-start = (bf16[2,4,256,256]{3,2,1,0:T(8,128)(2,1)S(1)}, bf16[2,4,256,256]{3,2,1,0:T(8,128)(2,1)}, u32[]{:S(2)}) copy-start(bf16[2,4,256,256]{3,2,1,0:T(8,128)(2,1)} %constant.7.clone.table_ref) | copy-start | bytes 3145732

commit v6 on v5

--- a/solution.py
+++ b/solution.py
@@ -410,8 +410,12 @@
         out_ref[y * span : (y + 1) * span, :] = all_ref[pl.ds(first, span), :]
 
 
-def solve_kernel(table, decay_ref, hat_ref, enter_ref, out_ref, work_ref, rows_ref):
+def solve_kernel(
+    table, decay_ref, hat_ref, enter_ref, conc_ref, out_ref, conc_hbm, work_ref, rows_ref, sem
+):
     n_gz, n_section, n_z, rows, _ = out_ref.shape
+    conc_copy = pltpu.make_async_copy(conc_ref.at[0], conc_hbm.at[0], sem)
+    conc_copy.start()
     depth = n_gz * n_z
     r = decay_ref[0]
     inverse = decay_ref[1]
@@ -429,10 +433,14 @@
         planes = [rows_ref[i, pl.ds(k * rows, rows), :] for k in range(depth)]
         for (g, q), plane in zip(where, sine_rows_back(planes, table)):
             out_ref[g, i, q] = plane
-
-
-def final_kernel(solved_ref, table_ref, conc_ref, out_hbm, conc_hbm, out_ref, sems, conc_sem):
-    conc_copy = pltpu.make_async_copy(conc_ref, conc_hbm, conc_sem)
+    conc_copy.wait()
+
+
+def final_kernel(
+    solved_ref, table_ref, conc_ref, _, out_hbm, conc_hbm, out_ref, sems, conc_sem
+):
+    rest = pl.ds(1, conc_ref.shape[0] - 1)
+    conc_copy = pltpu.make_async_copy(conc_ref.at[rest], conc_hbm.at[rest], conc_sem)
     conc_copy.start()
     n_gz, n_section, n_z, rows, _ = solved_ref.shape
     z_far = far_layer(n_z)
@@ -574,18 +582,22 @@
     )
     enter = enter.reshape(2 * n_section * depth, lanes)
 
-    solved = pl.pallas_call(
+    solved, conc_out = pl.pallas_call(
         functools.partial(solve_kernel, sine),
-        out_shape=jax.ShapeDtypeStruct((n_gz, n_section, n_z, rows, lanes), f32),
-        in_specs=[vmem] * 3,
-        out_specs=vmem,
+        out_shape=(
+            jax.ShapeDtypeStruct((n_gz, n_section, n_z, rows, lanes), f32),
+            jax.ShapeDtypeStruct(conc_section.shape, f32),
+        ),
+        in_specs=[vmem] * 4,
+        out_specs=(vmem, hbm),
         scratch_shapes=[
             pltpu.VMEM((rows, depth, lanes), f32),
             pltpu.VMEM((n_section, depth * rows, lanes), f32),
+            pltpu.SemaphoreType.DMA(()),
         ],
         compiler_params=params(12),
         name="solve",
-    )(decay_here, hat, enter)
+    )(decay_here, hat, enter, conc_new)
     returned = lax.all_to_all(solved, "gz", split_axis=0, concat_axis=0, tiled=True)
 
     potential_new, conc_new = pl.pallas_call(
@@ -594,7 +606,8 @@
             jax.ShapeDtypeStruct(potential.shape, f32),
             jax.ShapeDtypeStruct(conc_section.shape, f32),
         ),
-        in_specs=[vmem] * 3,
+        in_specs=[vmem] * 3 + [hbm],
+        input_output_aliases={3: 1},
         out_specs=(hbm, hbm),
         scratch_shapes=[
             pltpu.VMEM(potential.shape, f32),
@@ -603,7 +616,7 @@
         ],
         compiler_params=params(12),
         name="back_to_y",
-    )(returned, table_back, conc_new)
+    )(returned, table_back, conc_new, conc_out)
     return (conc_new, potential_new)
 
 

time: 97.3 us -> 97.6 us (level)
  no operation moved by 1% of the time
where the time goes in v6:
time: 97.6 us; the launch traced here: 97.3 us
  blocking collectives  64 us (66%)
  starting transfers between devices  22.1 us (23%)
  Pallas kernels  9.33 us (10%)
  waiting for transfers between devices  1.06 us (1%)
    all_to_all x1, blocking collectives, on_device(): lax.all_to_all(sums, 'xy', split_axis=0, concat_axis=0, tiled=True)  23.8 us
    ppermute x4, starting transfers between devices, swap(): return lax.ppermute(value, axis, pairs + [(j, i) for i, j in pairs])  22.1 us
    all_to_all x1, blocking collectives, on_device(): lax.all_to_all(solved, 'gz', split_axis=0, concat_axis=0, tiled=True)  13.9 us
    all_to_all x1, blocking collectives, on_device(): lax.all_to_all(modes, 'gz', split_axis=0, concat_axis=0, tiled=True)  13.6 us
    all_to_all x1, blocking collectives, on_device(): lax.all_to_all(entering, 'xy', split_axis=0, concat_axis=0, tiled=True, a...  12.8 us
    pallas_call x1, Pallas kernels, on_device(): pl.pallas_call(inner_kernel, out_shape=(jax.ShapeDtypeStruct(planes, f32)...  3.11 us
    pallas_call x1, Pallas kernels, on_device(): pl.pallas_call(outer_kernel, out_shape=(pltpu.VMEM(conc_section.shape, f3...  2.11 us
  transfers between devices with their start and end apart: 4, of which 1 were waited for; matrix products, arithmetic and copies ran while one was open for 0% of the time, Pallas kernels for 3%

profile of v6, /device:TPU:1, one launch (start us, length us, event | category | flops | bytes accessed | tf_op | source)
XLA Modules:
  0.0 97.3 jit_solution(4230180864228242015)
XLA Ops:
  0.6 0.0 copy-start.3
  0.6 0.0 copy-start.5
  0.7 0.0 copy-start.4
  0.7 0.0 copy-start.2
  0.7 1.7 %pack.1 = (f32[3,5,16,1024]{3,2,1,0:T(8,128)S(1)}, f32[3,5,16,1024]{3,2,1,0:T(8,128)S(1)}, f32[30,1024]{1,0:T(8,128)S(1)}, f32[30,1024]{1,0:T(8,128)S(1)}) custom-call(f32[3,4,2,16,1024]{4,3,2,1,0:T(8,128)} %conc_hbm.1, f32[3,2,16,1024]{3,2,1,0:T(8,128)} %pot_hbm.1), custom_call_target="tpu_custom_call" | custom-call | tf_op jit(solution)/shard_map/pack/pallas_call | solution.py:484
  2.3 0.0 copy-start.1
  2.3 4.6 %collective-permute-start = (f32[3,5,16,1024]{3,2,1,0:T(8,128)S(1)}, f32[3,5,16,1024]{3,2,1,0:T(8,128)S(1)}, u32[]{:S(2)}, u32[]{:S(2)}) collective-permute-start(f32[3,5,16,1024]{3,2,1,0:T(8,128)S(1)} %get-tuple-element.18.z_far_ref), channel_id=1, source_target_pairs={{1,2},{3,4},{5,6},{2,1},{4,3},{6,5},{9,10},{11,12},{13,14},{10,9},... | collective-permute-start | bytes 2949128 | tf_op jit(solution)/shard_map/ppermute | solution.py:498
  7.0 5.0 %collective-permute-start.3 = (f32[3,5,16,1024]{3,2,1,0:T(8,128)S(1)}, f32[3,5,16,1024]{3,2,1,0:T(8,128)S(1)}, u32[]{:S(2)}, u32[]{:S(2)}) collective-permute-start(f32[3,5,16,1024]{3,2,1,0:T(8,128)S(1)} %get-tuple-element.19.z_near_ref), channel_id=1, source_target_pairs={{0,1},{2,3},{4,5},{6,7},{1,0},{3,2},{5,4},{7,6},{8,9},{10,11},{12,... | collective-permute-start | bytes 2949128 | tf_op jit(solution)/shard_map/ppermute | solution.py:498
  12.0 10.5 %collective-permute-start.1 = (f32[30,1024]{1,0:T(8,128)S(1)}, f32[30,1024]{1,0:T(8,128)S(1)}, u32[]{:S(2)}, u32[]{:S(2)}) collective-permute-start(f32[30,1024]{1,0:T(8,128)S(1)} %get-tuple-element.23.x_far_sent), channel_id=1, source_target_pairs={{8,16},{24,32},{40,48},{56,64},{72,80},{88,96},{104,112},{120,128}... | collective-permute-start | bytes 368648 | tf_op jit(solution)/shard_map/ppermute | solution.py:498
  22.5 1.9 %collective-permute-start.2 = (f32[30,1024]{1,0:T(8,128)S(1)}, f32[30,1024]{1,0:T(8,128)S(1)}, u32[]{:S(2)}, u32[]{:S(2)}) collective-permute-start(f32[30,1024]{1,0:T(8,128)S(1)} %get-tuple-element.24.x_near_sent), channel_id=1, source_target_pairs={{0,8},{16,24},{32,40},{48,56},{64,72},{80,88},{96,104},{112,120},{... | collective-permute-start | bytes 368648 | tf_op jit(solution)/shard_map/ppermute | solution.py:498
  24.5 3.1 %inner_faces.1 = (f32[3,4,2,16,1024]{4,3,2,1,0:T(8,128)S(1)}, f32[3,2,16,1024]{3,2,1,0:T(8,128)S(1)}, f32[3,16,128]{2,1,0:T(8,128)S(1)}, f32[2,128]{1,0:T(2,128)S(1)}) custom-call(f32[4]{0:T(128)S(1)} %copy-done.4, s32[4]{0:T(128)S(1)} %copy-done.5, f32[4,2,16,1024]{3,2,1,0:T(8,128)S(1)} %copy-done.2, f32[3,5,16,1024]{3,2,1,0:T(8,128)S(1)} %get-tuple-element.18.z_far_ref, ...), custom_call_target="tpu_custom_call" | custom-call | flops 20000000 | bytes 4500000 | tf_op jit(solution)/shard_map/inner_faces/pallas_call | solution.py:507
  27.6 0.0 collective-permute-done.1.x_far_got
  27.6 1.1 %collective-permute-done.2.x_near_got = f32[30,1024]{1,0:T(8,128)S(1)} collective-permute-done((f32[30,1024]{1,0:T(8,128)S(1)}, f32[30,1024]{1,0:T(8,128)S(1)}, u32[]{:S(2)}, u32[]{:S(2)}) %collective-permute-start.2) | collective-permute-done | bytes 122912 | tf_op jit(solution)/shard_map/ppermute | solution.py:498
  28.6 0.0 collective-permute-done.z_far_got
  28.6 0.0 collective-permute-done.3.z_near_got
  28.7 2.1 %outer_faces.1 = (f32[3,4,2,16,1024]{4,3,2,1,0:T(8,128)S(1)}, f32[8,96,128]{2,1,0:T(8,128)S(1)}) custom-call(f32[4]{0:T(128)S(1)} %copy-done.4, s32[4]{0:T(128)S(1)} %copy-done.5, f32[3,4,2,16,1024]{4,3,2,1,0:T(8,128)S(1)} %get-tuple-element.21.part_ref, f32[3,2,16,1024]{3,2,1,0:T(8,128)S(1)} %get-tuple-element.22.rhs_part_ref, ...), custom_call_target="tpu_custom_call" | custom-call | tf_op jit(solution)/shard_map/outer_faces/pallas_call | solution.py:526
  30.8 13.6 %all_to_all.20 = f32[8,96,128]{2,1,0:T(8,128)S(1)} all-to-all(f32[8,96,128]{2,1,0:T(8,128)S(1)} %get-tuple-element.25), channel_id=1, replica_groups=mesh['xy'=64,'gz'=8] {'gz'}, dimensions={0} | all-to-all | bytes 786432 | tf_op jit(solution)/shard_map/all_to_all | solution.py:546
  44.3 0.4 block_sums.1
  44.7 23.8 %all_to_all.21 = f32[64,3,2,128]{3,2,1,0:T(2,128)S(1)} all-to-all(f32[64,3,2,128]{3,2,1,0:T(2,128)S(1)} %bitcast.7), channel_id=1, replica_groups=mesh['xy'=64,'gz'=8] {'xy'}, dimensions={0} | all-to-all | bytes 393216 | tf_op jit(solution)/shard_map/all_to_all | solution.py:564
  68.5 0.1 ring.1
  68.6 12.8 %all_to_all.22 = f32[16,3,2,128]{3,2,1,0:T(2,128)S(1)} all-to-all(f32[16,3,2,128]{3,2,1,0:T(2,128)S(1)} %bitcast.8), channel_id=1, replica_groups={{0,8,16,24,128,136,144,152,256,264,272,280,384,392,400,408},{32,40,48,5..., dimensions={0} | all-to-all | bytes 98304 | tf_op jit(solution)/shard_map/all_to_all | solution.py:580
  81.4 0.8 solve.1
  82.2 13.9 %all_to_all.23.solved_ref = f32[8,3,2,16,128]{4,3,2,1,0:T(8,128)S(1)} all-to-all(f32[8,3,2,16,128]{4,3,2,1,0:T(8,128)S(1)} %get-tuple-element.30), channel_id=1, replica_groups=mesh['xy'=64,'gz'=8] {'gz'}, dimensions={0} | all-to-all | bytes 786432 | tf_op jit(solution)/shard_map/all_to_all | solution.py:601
  96.1 1.2 %back_to_y.1 = (f32[3,2,16,1024]{3,2,1,0:T(8,128)}, f32[3,4,2,16,1024]{4,3,2,1,0:T(8,128)}) custom-call(f32[8,3,2,16,128]{4,3,2,1,0:T(8,128)S(1)} %all_to_all.23.solved_ref, bf16[2,4,256,256]{3,2,1,0:T(8,128)(2,1)S(1)} %copy-done, f32[3,4,2,16,1024]{4,3,2,1,0:T(8,128)S(1)} %get-tuple-element.29.conc_ref, ...), custom_call_target="tpu_custom_call", output_to_operand_aliasing={{1}: (3, {})} | custom-call | tf_op jit(solution)/shard_map/back_to_y/pallas_call | solution.py:603
  (7 shorter events, 0.0 us)
Async XLA Ops:
  0.6 23.8 %copy-start.3 = (f32[24,128]{1,0:T(8,128)S(1)}, f32[24,128]{1,0:T(8,128)}, u32[]{:S(2)}) copy-start(f32[24,128]{1,0:T(8,128)} %constant.8.clone.wave_ref) | copy-start | bytes 36868
  0.6 23.8 %copy-start.5 = (s32[4]{0:T(128)S(1)}, s32[4]{0:T(128)}, u32[]{:S(2)}) copy-start(s32[4]{0:T(128)} %charge_ref.3) | copy-start | bytes 52
  0.7 23.8 %copy-start.4 = (f32[4]{0:T(128)S(1)}, f32[4]{0:T(128)}, u32[]{:S(2)}) copy-start(f32[4]{0:T(128)} %diffusivity_ref.3) | copy-start | bytes 52
  0.7 23.8 %copy-start.2 = (f32[4,2,16,1024]{3,2,1,0:T(8,128)S(1)}, f32[4,2,16,1024]{3,2,1,0:T(8,128)}, u32[]{:S(2)}) copy-start(f32[4,2,16,1024]{3,2,1,0:T(8,128)} %prev_ref.1) | copy-start | bytes 1572868
  2.3 26.3 %copy-start.1 = (bf16[2,4,256,256]{3,2,1,0:T(8,128)(2,1)S(1)}, bf16[2,4,256,256]{3,2,1,0:T(8,128)(2,1)}, u32[]{:S(2)}) copy-start(bf16[2,4,256,256]{3,2,1,0:T(8,128)(2,1)} %constant.6.clone.table_ref) | copy-start | bytes 3145732
  2.3 26.3 %collective-permute-start = (f32[3,5,16,1024]{3,2,1,0:T(8,128)S(1)}, f32[3,5,16,1024]{3,2,1,0:T(8,128)S(1)}, u32[]{:S(2)}, u32[]{:S(2)}) collective-permute-start(f32[3,5,16,1024]{3,2,1,0:T(8,128)S(1)} %get-tuple-element.18.z_far_ref), channel_id=1, source_target_pairs={{1,2},{3,4},{5,6},{2,1},{4,3},{6,5},{9,10},{11,12},{13,14},{10,9},... | collective-permute-start | bytes 2949128 | tf_op jit(solution)/shard_map/ppermute | solution.py:498
  7.0 21.7 %collective-permute-start.3 = (f32[3,5,16,1024]{3,2,1,0:T(8,128)S(1)}, f32[3,5,16,1024]{3,2,1,0:T(8,128)S(1)}, u32[]{:S(2)}, u32[]{:S(2)}) collective-permute-start(f32[3,5,16,1024]{3,2,1,0:T(8,128)S(1)} %get-tuple-element.19.z_near_ref), channel_id=1, source_target_pairs={{0,1},{2,3},{4,5},{6,7},{1,0},{3,2},{5,4},{7,6},{8,9},{10,11},{12,... | collective-permute-start | bytes 2949128 | tf_op jit(solution)/shard_map/ppermute | solution.py:498
  12.0 15.6 %collective-permute-start.1 = (f32[30,1024]{1,0:T(8,128)S(1)}, f32[30,1024]{1,0:T(8,128)S(1)}, u32[]{:S(2)}, u32[]{:S(2)}) collective-permute-start(f32[30,1024]{1,0:T(8,128)S(1)} %get-tuple-element.23.x_far_sent), channel_id=1, source_target_pairs={{8,16},{24,32},{40,48},{56,64},{72,80},{88,96},{104,112},{120,128}... | collective-permute-start | bytes 368648 | tf_op jit(solution)/shard_map/ppermute | solution.py:498
  22.5 6.1 %collective-permute-start.2 = (f32[30,1024]{1,0:T(8,128)S(1)}, f32[30,1024]{1,0:T(8,128)S(1)}, u32[]{:S(2)}, u32[]{:S(2)}) collective-permute-start(f32[30,1024]{1,0:T(8,128)S(1)} %get-tuple-element.24.x_near_sent), channel_id=1, source_target_pairs={{0,8},{16,24},{32,40},{48,56},{64,72},{80,88},{96,104},{112,120},{... | collective-permute-start | bytes 368648 | tf_op jit(solution)/shard_map/ppermute | solution.py:498
  68.5 27.6 %copy-start = (bf16[2,4,256,256]{3,2,1,0:T(8,128)(2,1)S(1)}, bf16[2,4,256,256]{3,2,1,0:T(8,128)(2,1)}, u32[]{:S(2)}) copy-start(bf16[2,4,256,256]{3,2,1,0:T(8,128)(2,1)} %constant.7.clone.table_ref) | copy-start | bytes 3145732
